TPU v7x, 32 devices: a whole 2x2x4 slice. The times are simulated.
32 devices in a mesh: ctx: 8 (over z, x), tp: 4 (over y, core).
Axes of the slice: x: 2, y: 2, z: 4, core: 2. Of those that a mesh axis runs over, the one named last changes fastest.
Arguments:
- queries: bfloat16 [8192, 4096], P(('ctx', 'tp')), may hold values from -40 to 40
- keys_in: bfloat16 [8192, 1024], P(('ctx', 'tp')), may hold values from -4 to 4
- values_in: bfloat16 [8192, 1024], P(('ctx', 'tp')), may hold values from -6 to 6
- grad_output: bfloat16 [8192, 4096], P(('ctx', 'tp')), may hold values from -6 to 6
- beacon_keys: bfloat16 [1024, 1024], P('ctx', 'tp'), may hold values from -6 to 6
- beacon_values: bfloat16 [1024, 1024], P('ctx', 'tp'), may hold values from -6 to 6
- read_blocks: int32 [8, 4], P('ctx'), may hold values from 0 to 6, as said below
- read_counts: int32 [8], P('ctx'), may hold values from 0 to 4, as said below
Outputs:
- attn_out: bfloat16 [8192, 4096], P(('ctx', 'tp'))
- grad_queries: bfloat16 [8192, 4096], P(('ctx', 'tp'))
- grad_keys: bfloat16 [8192, 1024], P(('ctx', 'tp'))
- grad_values: bfloat16 [8192, 1024], P(('ctx', 'tp'))
- grad_beacon_keys: bfloat16 [1024, 1024], P('ctx', 'tp')
- grad_beacon_values: bfloat16 [1024, 1024], P('ctx', 'tp')
Inputs may be any that keep to these rules, and one draw needn't show every extreme that they name: `read_blocks`: row s lists distinct blocks of earlier segments in its first read_counts[s] slots, block s - 1 first; unused slots hold 0. The last segment reads block 3 in its second slot. read_counts[s] is at most min(s, 4); segment 0 reads nothing and the last segment uses all 4 slots.
All inputs are finite; a program needn't handle non-finite values.
Results may differ from a plain program's by a relative error of at most 0.01.
Values may be sent and summed in bfloat16 or wider, within the bound.
A program may use at most 128 MiB of HBM per device.

v0:
```python
import jax
import jax.numpy as jnp
from jax import lax
from jax.sharding import PartitionSpec as P

HD = 128


def shifted(value, axis, by):
    peers = lax.axis_size(axis)
    pairs = [(i, i + by) for i in range(peers) if 0 <= i + by < peers]
    return lax.ppermute(value, axis, pairs)


def head_grads(query_rows, key_rows, value_rows, grad_rows, allowed, score_scale):
    scores = jnp.dot(query_rows, key_rows.T, preferred_element_type=jnp.float32) * score_scale
    scores = jnp.where(allowed, scores, -1e30)
    row_max = jnp.max(scores, axis=1, keepdims=True)
    weights = jnp.exp(scores - row_max)
    prob_full = weights / jnp.sum(weights, axis=1, keepdims=True)
    prob_half = prob_full.astype(jnp.bfloat16)
    output = jnp.dot(prob_half, value_rows, preferred_element_type=jnp.float32).astype(jnp.bfloat16)
    grad_prob = jnp.dot(grad_rows, value_rows.T, preferred_element_type=jnp.float32)
    row_delta = jnp.sum(
        grad_rows.astype(jnp.float32) * output.astype(jnp.float32), axis=1, keepdims=True
    )
    dscores = (prob_full * (grad_prob - row_delta) * score_scale).astype(jnp.bfloat16)
    grad_query = jnp.dot(dscores, key_rows, preferred_element_type=jnp.float32).astype(jnp.bfloat16)
    grad_key = jnp.dot(dscores.T, query_rows, preferred_element_type=jnp.float32)
    grad_value = jnp.dot(prob_half.T, grad_rows, preferred_element_type=jnp.float32)
    return (output, grad_query, grad_key, grad_value)


def shards(
    queries, keys_in, values_in, grad_output, beacon_keys, beacon_values, read_blocks, read_counts
):
    seg_q, seg_k, seg_v, seg_g = (
        lax.all_to_all(queries, "tp", split_axis=1, concat_axis=0, tiled=True),
        lax.all_to_all(keys_in, "tp", split_axis=1, concat_axis=0, tiled=True),
        lax.all_to_all(values_in, "tp", split_axis=1, concat_axis=0, tiled=True),
        lax.all_to_all(grad_output, "tp", split_axis=1, concat_axis=0, tiled=True),
    )
    all_k, all_v = (
        lax.all_gather(beacon_keys, "ctx", axis=0, tiled=True),
        lax.all_gather(beacon_values, "ctx", axis=0, tiled=True),
    )
    seg_len = seg_q.shape[0]
    head_count = seg_q.shape[1] // HD
    kv_heads = seg_k.shape[1] // HD
    group_size = head_count // kv_heads
    col_width = seg_k.shape[1]
    block_rows = beacon_keys.shape[0]
    owners = lax.axis_size("ctx")
    read_row = read_blocks[0]
    read_count = read_counts[0]
    read_slots = read_row.shape[0]
    beacon_rows = read_slots * block_rows
    score_scale = HD ** (-0.5)
    positions = jnp.arange(seg_len, dtype=jnp.int32)
    causal = positions[None, :] <= positions[:, None]
    slot_ok = jnp.arange(read_slots, dtype=jnp.int32) < read_count
    valid_keys = jnp.repeat(slot_ok, block_rows)
    allowed = jnp.concatenate(
        [causal, jnp.broadcast_to(valid_keys[None, :], (seg_len, beacon_rows))], axis=1
    )
    chosen_k = jnp.take(all_k.reshape(owners, block_rows, col_width), read_row, axis=0).reshape(
        beacon_rows, col_width
    )
    chosen_v = jnp.take(all_v.reshape(owners, block_rows, col_width), read_row, axis=0).reshape(
        beacon_rows, col_width
    )
    query_heads = seg_q.reshape(seg_len, head_count, HD).transpose(1, 0, 2)
    grad_heads = seg_g.reshape(seg_len, head_count, HD).transpose(1, 0, 2)
    key_heads = (
        jnp.concatenate([seg_k, chosen_k], axis=0)
        .reshape(seg_len + beacon_rows, kv_heads, HD)
        .transpose(1, 0, 2)
    )
    value_heads = (
        jnp.concatenate([seg_v, chosen_v], axis=0)
        .reshape(seg_len + beacon_rows, kv_heads, HD)
        .transpose(1, 0, 2)
    )

    def per_head(head_index):
        shared = head_index // group_size
        return head_grads(
            query_heads[head_index],
            key_heads[shared],
            value_heads[shared],
            grad_heads[head_index],
            allowed,
            score_scale,
        )

    outputs, grad_query, grad_key, grad_value = lax.map(
        per_head, jnp.arange(head_count, dtype=jnp.int32)
    )
    grad_key = jnp.sum(grad_key.reshape(kv_heads, group_size, seg_len + beacon_rows, HD), axis=1)
    grad_value = jnp.sum(
        grad_value.reshape(kv_heads, group_size, seg_len + beacon_rows, HD), axis=1
    )
    local_k = (
        grad_key[:, :seg_len].transpose(1, 0, 2).reshape(seg_len, col_width).astype(jnp.bfloat16)
    )
    local_v = (
        grad_value[:, :seg_len].transpose(1, 0, 2).reshape(seg_len, col_width).astype(jnp.bfloat16)
    )
    part_k = grad_key[:, seg_len:].transpose(1, 0, 2).reshape(read_slots, block_rows, col_width)
    part_v = grad_value[:, seg_len:].transpose(1, 0, 2).reshape(read_slots, block_rows, col_width)
    slot_weight = slot_ok.astype(jnp.float32)
    first_k = part_k[0] * slot_weight[0]
    first_v = part_v[0] * slot_weight[0]
    near_k, near_v = (
        shifted(first_k.astype(jnp.bfloat16), "ctx", -1).astype(first_k.dtype),
        shifted(first_v.astype(jnp.bfloat16), "ctx", -1).astype(first_v.dtype),
    )
    later_k = (part_k[1:] * slot_weight[1:, None, None])[None]
    later_v = (part_v[1:] * slot_weight[1:, None, None])[None]
    targets = jnp.where(slot_ok[1:], read_row[1:], -1).astype(jnp.float32)[None]
    my_block = lax.axis_index("ctx").astype(jnp.float32)
    empty = jnp.zeros((block_rows, col_width), jnp.float32)
    piece_k = lax.all_gather(later_k.astype(jnp.bfloat16), "ctx", axis=0, tiled=True).astype(
        jnp.float32
    )
    piece_v = lax.all_gather(later_v.astype(jnp.bfloat16), "ctx", axis=0, tiled=True).astype(
        jnp.float32
    )
    piece_t = lax.all_gather(targets.astype(jnp.bfloat16), "ctx", axis=0, tiled=True).astype(
        jnp.float32
    )
    match = (piece_t == my_block).astype(jnp.float32)
    add_k = jnp.einsum("nj,njrc->rc", match, piece_k, precision=lax.Precision.HIGHEST)
    add_v = jnp.einsum("nj,njrc->rc", match, piece_v, precision=lax.Precision.HIGHEST)
    far_k = empty + add_k
    far_v = empty + add_v
    own_k = near_k + far_k
    own_v = near_v + far_v
    seg_out = outputs.transpose(1, 0, 2).reshape(seg_len, head_count * HD)
    seg_gq = grad_query.transpose(1, 0, 2).reshape(seg_len, head_count * HD)
    tok_out, tok_gq, tok_gk, tok_gv = (
        lax.all_to_all(seg_out, "tp", split_axis=0, concat_axis=1, tiled=True),
        lax.all_to_all(seg_gq, "tp", split_axis=0, concat_axis=1, tiled=True),
        lax.all_to_all(local_k, "tp", split_axis=0, concat_axis=1, tiled=True),
        lax.all_to_all(local_v, "tp", split_axis=0, concat_axis=1, tiled=True),
    )
    return (tok_out, tok_gq, tok_gk, tok_gv, own_k.astype(jnp.bfloat16), own_v.astype(jnp.bfloat16))


def solution(mesh):
    in_specs = (
        P(("ctx", "tp"), None),
        P(("ctx", "tp"), None),
        P(("ctx", "tp"), None),
        P(("ctx", "tp"), None),
        P("ctx", "tp"),
        P("ctx", "tp"),
        P("ctx", None),
        P("ctx"),
    )
    out_specs = (
        P(("ctx", "tp"), None),
        P(("ctx", "tp"), None),
        P(("ctx", "tp"), None),
        P(("ctx", "tp"), None),
        P("ctx", "tp"),
        P("ctx", "tp"),
    )
    return jax.shard_map(shards, mesh=mesh, in_specs=in_specs, out_specs=out_specs, check_vma=False)
```

profile of v0, /device:TPU:12, one launch (start us, length us, event | category | flops | bytes accessed | tf_op | source)
XLA Modules:
  0.0 468.9 jit_solution(1208707042547626975)
XLA Ops:
  9.2 3.9 all-to-all-start.1
  15.0 5.3 %all-to-all-done.1 = bf16[256,4,256]{2,0,1:T(8,128)(2,1)S(1)} async-done(((bf16[256,4,256]{2,0,1:T(8,128)(2,1)}), bf16[256,4,256]{2,0,1:T(8,128)(2,1)S(1)}, u32[]{:S(2)}, u32[]{:S(2)}) %all-to-all-start.1) | async-done | bytes 524320 | tf_op jit(solution)/shard_map/all_to_all | solution.py:39
  20.3 5.1 %all-to-all-start.2 = ((bf16[256,4,256]{2,0,1:T(8,128)(2,1)}), bf16[256,4,256]{2,0,1:T(8,128)(2,1)S(1)}, u32[]{:S(2)}, u32[]{:S(2)}) async-start(bf16[256,4,256]{2,0,1:T(8,128)(2,1)} %bitcast.172), calls=%async_computation.2 | async-start | bytes 1048576 | tf_op jit(solution)/shard_map/all_to_all | solution.py:40
  28.0 4.7 all-to-all-done.2
  32.6 5.2 %all-to-all-start.3 = ((bf16[256,4,1024]{0,2,1:T(8,128)(2,1)}), bf16[256,4,1024]{0,2,1:T(8,128)(2,1)S(1)}, u32[]{:S(2)}, u32[]{:S(2)}) async-start(bf16[256,4,1024]{0,2,1:T(8,128)(2,1)} %bitcast.161), calls=%async_computation.3 | async-start | bytes 4194304 | tf_op jit(solution)/shard_map/all_to_all | solution.py:41
  37.9 30.9 %all_gather.15 = bf16[1024,256]{1,0:T(8,128)(2,1)} all-gather(bf16[128,256]{1,0:T(8,128)(2,1)S(1)} %copy-done.4), channel_id=1, replica_groups=mesh['ctx'=8,'tp'=4] {'ctx'}, dimensions={0}, use_global_device_ids=true | all-gather | bytes 589824 | tf_op jit(solution)/shard_map/all_gather | solution.py:44
  70.4 33.4 %all_gather.16 = bf16[1024,256]{1,0:T(8,128)(2,1)} all-gather(bf16[128,256]{1,0:T(8,128)(2,1)S(1)} %copy-done.5), channel_id=1, replica_groups=mesh['ctx'=8,'tp'=4] {'ctx'}, dimensions={0}, use_global_device_ids=true | all-gather | bytes 589824 | tf_op jit(solution)/shard_map/all_gather | solution.py:45
  106.1 3.1 copy.109
  109.3 4.5 all-to-all-start
  120.9 5.9 %maximum_bitcast_fusion = bf16[2,1536,128]{2,0,1:T(2,128)(2,1)S(1)} fusion(bf16[512,2,128]{2,1,0:T(2,128)(2,1)S(1)} %concatenate.20, bf16[1024,2,128]{2,1,0:T(2,128)(2,1)S(1)} %concatenate.19), kind=kLoop, calls=%fused_computation.51 | loop fusion | flops 393216 | bytes 1572864 | tf_op jit(solution)/shard_map/transpose | solution.py:77
  127.0 3.6 maximum_bitcast_fusion.1
  130.8 4.0 copy.61
  134.8 3.6 copy.105
  138.4 4.1 copy.66
  146.4 184.9 %while.18 = (s32[]{:T(128)}, bf16[8,1024,128]{1,2,0:T(8,128)(2,1)}, bf16[8,1024,128]{2,1,0:T(8,128)(2,1)}, f32[8,1536,128]{2,1,0:T(8,128)}, f32[8,1536,128]{2,1,...) while((s32[]{:T(128)}, bf16[8,1024,128]{1,2,0:T(8,128)(2,1)}, ...), condition=%wide.region_4.6_spmd, body=%wide.region_0.5_spmd.sunk | while | flops 2443441152 | bytes 48019868 | solution.py:96
  154.2 3.8 fusion.71
  161.7 3.2 multiply_convert_fusion.4
  177.3 3.7 fusion.71
  184.8 3.2 multiply_convert_fusion.4
  188.0 2.9 fusion.70
  200.5 3.8 fusion.71
  208.0 3.2 multiply_convert_fusion.4
  223.6 3.8 fusion.71
  231.1 3.2 multiply_convert_fusion.4
  246.8 3.7 fusion.71
  254.2 3.2 multiply_convert_fusion.4
  269.8 3.7 fusion.71
  277.3 3.2 multiply_convert_fusion.4
  292.9 3.7 fusion.71
  300.4 3.2 multiply_convert_fusion.4
  316.0 3.7 fusion.71
  323.5 3.2 multiply_convert_fusion.4
  331.3 3.3 bitcast_reduce_fusion.1
  336.0 3.3 bitcast_reduce_fusion
  346.8 3.5 all-to-all-start.6
  352.1 5.4 %all-to-all-done.6 = bf16[4,256,256]{2,1,0:T(8,128)(2,1)S(1)} async-done(((bf16[4,256,256]{2,1,0:T(8,128)(2,1)}), bf16[4,256,256]{2,1,0:T(8,128)(2,1)S(1)}, u32[]{:S(2)}, u32[]{:S(2)}) %all-to-all-start.6) | async-done | bytes 524320 | tf_op jit(solution)/shard_map/all_to_all | solution.py:144
  357.5 5.8 %all-to-all-start.7 = ((bf16[4,256,256]{2,1,0:T(8,128)(2,1)}), bf16[4,256,256]{2,1,0:T(8,128)(2,1)}, u32[]{:S(2)}, u32[]{:S(2)}) async-start(bf16[4,256,256]{2,1,0:T(8,128)(2,1)} %convert_element_type.122), calls=%async_computation.7 | async-start | bytes 1048576 | tf_op jit(solution)/shard_map/all_to_all | solution.py:145
  363.2 3.3 reshape.173
  366.6 3.0 copy.99
  370.5 6.1 %all-to-all-start.4 = ((bf16[4,256,1024]{2,1,0:T(8,128)(2,1)}), bf16[4,256,1024]{2,1,0:T(8,128)(2,1)}, u32[]{:S(2)}, u32[]{:S(2)}) async-start(bf16[4,256,1024]{2,1,0:T(8,128)(2,1)} %copy.99), calls=%async_computation.4 | async-start | bytes 4194304 | tf_op jit(solution)/shard_map/all_to_all | solution.py:142
  377.3 3.0 copy.69
  382.6 18.1 %all-to-all-done.4 = bf16[4,256,1024]{2,1,0:T(8,128)(2,1)} async-done(((bf16[4,256,1024]{2,1,0:T(8,128)(2,1)}), bf16[4,256,1024]{2,1,0:T(8,128)(2,1)}, u32[]{:S(2)}, u32[]{:S(2)}) %all-to-all-start.4) | async-done | bytes 2097184 | tf_op jit(solution)/shard_map/all_to_all | solution.py:142
  400.7 5.2 %all-to-all-start.5 = ((bf16[4,256,1024]{2,1,0:T(8,128)(2,1)}), bf16[4,256,1024]{2,1,0:T(8,128)(2,1)S(1)}, u32[]{:S(2)}, u32[]{:S(2)}) async-start(bf16[4,256,1024]{2,1,0:T(8,128)(2,1)} %all_to_all.116), calls=%async_computation.5 | async-start | bytes 4194304 | tf_op jit(solution)/shard_map/all_to_all | solution.py:143
  407.5 21.8 %all-reduce = bf16[24]{0:T(256)(128)(2,1)S(1)} all-reduce(bf16[24]{0:T(256)(128)(2,1)S(1)} %dynamic-update-slice), channel_id=2, replica_groups=mesh['ctx'=8,'tp'=4] {'ctx'}, use_global_device_ids=true, to_apply=%add | all-reduce | flops 24 | bytes 96
  432.0 6.6 %collective-permute-start = (bf16[128,256]{0,1:T(8,128)(2,1)S(1)}, bf16[128,256]{0,1:T(8,128)(2,1)S(1)}, u32[]{:S(2)}, u32[]{:S(2)}) collective-permute-start(bf16[128,256]{0,1:T(8,128)(2,1)S(1)} %bitcast.179), channel_id=1, source_target_pairs={{4,0},{8,4},{12,8},{16,12},{20,16},{24,20},{28,24},{5,1},{9,5},{13... | collective-permute-start | bytes 196616 | tf_op jit(solution)/shard_map/ppermute | solution.py:12
  443.1 3.9 copy.68
  447.0 4.1 copy.79
  453.7 4.1 copy.80
  (163 shorter events, 145.3 us)
Async XLA Ops:
  7.2 18.3 %copy-start.2 = (bf16[256,4096]{1,0:T(8,128)(2,1)S(1)}, bf16[256,4096]{1,0:T(8,128)(2,1)}, u32[]{:S(2)}) copy-start(bf16[256,4096]{1,0:T(8,128)(2,1)} %param.15) | copy-start | bytes 6291460
  9.2 11.1 %all-to-all-start.1 = ((bf16[256,4,256]{2,0,1:T(8,128)(2,1)}), bf16[256,4,256]{2,0,1:T(8,128)(2,1)S(1)}, u32[]{:S(2)}, u32[]{:S(2)}) async-start(bf16[256,4,256]{2,0,1:T(8,128)(2,1)} %bitcast.123), calls=%async_computation.1 | async-start | bytes 1048576 | tf_op jit(solution)/shard_map/all_to_all | solution.py:39
  20.3 12.3 %all-to-all-start.2 = ((bf16[256,4,256]{2,0,1:T(8,128)(2,1)}), bf16[256,4,256]{2,0,1:T(8,128)(2,1)S(1)}, u32[]{:S(2)}, u32[]{:S(2)}) async-start(bf16[256,4,256]{2,0,1:T(8,128)(2,1)} %bitcast.172), calls=%async_computation.2 | async-start | bytes 1048576 | tf_op jit(solution)/shard_map/all_to_all | solution.py:40
  28.0 9.9 %copy-start.9 = (s32[1,4]{1,0:T(1,128)S(1)}, s32[1,4]{1,0:T(1,128)}, u32[]{:S(2)}) copy-start(s32[1,4]{1,0:T(1,128)} %param.18) | copy-start | bytes 52
  28.0 9.9 %copy-start.4 = (bf16[128,256]{1,0:T(8,128)(2,1)S(1)}, bf16[128,256]{1,0:T(8,128)(2,1)}, u32[]{:S(2)}) copy-start(bf16[128,256]{1,0:T(8,128)(2,1)} %param.16) | copy-start | bytes 196612
  28.0 42.4 %copy-start.5 = (bf16[128,256]{1,0:T(8,128)(2,1)S(1)}, bf16[128,256]{1,0:T(8,128)(2,1)}, u32[]{:S(2)}) copy-start(bf16[128,256]{1,0:T(8,128)(2,1)} %param.17) | copy-start | bytes 196612
  32.6 76.6 %all-to-all-start.3 = ((bf16[256,4,1024]{0,2,1:T(8,128)(2,1)}), bf16[256,4,1024]{0,2,1:T(8,128)(2,1)S(1)}, u32[]{:S(2)}, u32[]{:S(2)}) async-start(bf16[256,4,1024]{0,2,1:T(8,128)(2,1)} %bitcast.161), calls=%async_computation.3 | async-start | bytes 4194304 | tf_op jit(solution)/shard_map/all_to_all | solution.py:41
  109.2 9.1 %copy-start = (bf16[256,4,1024]{0,2,1:T(8,128)(2,1)}, bf16[256,4,1024]{0,2,1:T(8,128)(2,1)S(1)}, u32[]{:S(2)}) copy-start(bf16[256,4,1024]{0,2,1:T(8,128)(2,1)S(1)} %all-to-all-done.3) | copy-start | bytes 6291460
  109.3 33.2 %all-to-all-start = ((bf16[256,4,1024]{2,0,1:T(8,128)(2,1)}), bf16[256,4,1024]{2,0,1:T(8,128)(2,1)}, u32[]{:S(2)}, u32[]{:S(2)}) async-start(bf16[256,4,1024]{2,0,1:T(8,128)(2,1)} %bitcast.160), calls=%async_computation | async-start | bytes 4194304 | tf_op jit(solution)/shard_map/all_to_all | solution.py:38
  113.7 344.0 %all-gather.4.cloned.1.call-start = ((), (), s32[]{:S(2)}) async-start(), calls=%async_computation.8 | async-start | bytes 1769472 | tf_op jit(solution)/shard_map/all_gather | solution.py:123
  119.0 0.7 copy-start.6
  119.0 1.7 copy-start.12
  334.6 1.5 copy-start.1
  339.3 0.7 copy-start.8
  346.8 10.7 %all-to-all-start.6 = ((bf16[4,256,256]{2,1,0:T(8,128)(2,1)}), bf16[4,256,256]{2,1,0:T(8,128)(2,1)S(1)}, u32[]{:S(2)}, u32[]{:S(2)}) async-start(bf16[4,256,256]{2,1,0:T(8,128)(2,1)} %convert_element_type.120), calls=%async_computation.6 | async-start | bytes 1048576 | tf_op jit(solution)/shard_map/all_to_all | solution.py:144
  357.5 5.8 %copy-start.3 = (bf16[4,256,256]{2,1,0:T(8,128)(2,1)}, bf16[4,256,256]{2,1,0:T(8,128)(2,1)S(1)}, u32[]{:S(2)}) copy-start(bf16[4,256,256]{2,1,0:T(8,128)(2,1)S(1)} %all-to-all-done.6) | copy-start | bytes 1572868
  357.5 13.0 %all-to-all-start.7 = ((bf16[4,256,256]{2,1,0:T(8,128)(2,1)}), bf16[4,256,256]{2,1,0:T(8,128)(2,1)}, u32[]{:S(2)}, u32[]{:S(2)}) async-start(bf16[4,256,256]{2,1,0:T(8,128)(2,1)} %convert_element_type.122), calls=%async_computation.7 | async-start | bytes 1048576 | tf_op jit(solution)/shard_map/all_to_all | solution.py:145
  370.5 30.2 %all-to-all-start.4 = ((bf16[4,256,1024]{2,1,0:T(8,128)(2,1)}), bf16[4,256,1024]{2,1,0:T(8,128)(2,1)}, u32[]{:S(2)}, u32[]{:S(2)}) async-start(bf16[4,256,1024]{2,1,0:T(8,128)(2,1)} %copy.99), calls=%async_computation.4 | async-start | bytes 4194304 | tf_op jit(solution)/shard_map/all_to_all | solution.py:142
  376.6 81.1 %all-gather.6.cloned.1.call-start = ((), (), s32[]{:S(2)}) async-start(), calls=%async_computation.9 | async-start | bytes 1769472 | tf_op jit(solution)/shard_map/all_gather | solution.py:126
  382.6 23.4 %copy-start.11 = (u32[32]{0:T(128)S(1)}, u32[32]{0:T(128)}, u32[]{:S(2)}) copy-start(u32[32]{0:T(128)} %constant.102) | copy-start | bytes 388
  382.6 24.6 %copy-start.10 = (s32[1,4]{1,0:T(1,128)S(1)}, s32[1,4]{1,0:T(1,128)}, u32[]{:S(2)}) copy-start(s32[1,4]{1,0:T(1,128)} %param.18) | copy-start | bytes 52
  382.6 24.6 %copy-start.13 = (pred[4]{0:T(512)(128)(4,1)S(1)}, pred[4]{0:T(512)(128)(4,1)}, u32[]{:S(2)}) copy-start(pred[4]{0:T(512)(128)(4,1)} %copy-done.12) | copy-start | bytes 16
  382.6 46.8 %copy-start.7 = (f32[4]{0:T(128)S(1)}, f32[4]{0:T(128)}, u32[]{:S(2)}) copy-start(f32[4]{0:T(128)} %copy-done.6) | copy-start | bytes 52
  400.7 50.4 %all-to-all-start.5 = ((bf16[4,256,1024]{2,1,0:T(8,128)(2,1)}), bf16[4,256,1024]{2,1,0:T(8,128)(2,1)S(1)}, u32[]{:S(2)}, u32[]{:S(2)}) async-start(bf16[4,256,1024]{2,1,0:T(8,128)(2,1)} %all_to_all.116), calls=%async_computation.5 | async-start | bytes 4194304 | tf_op jit(solution)/shard_map/all_to_all | solution.py:143
  429.6 30.8 %collective-permute-start.1 = (bf16[128,256]{0,1:T(8,128)(2,1)S(1)}, bf16[128,256]{0,1:T(8,128)(2,1)S(1)}, u32[]{:S(2)}, u32[]{:S(2)}) collective-permute-start(bf16[128,256]{0,1:T(8,128)(2,1)S(1)} %bitcast.180), channel_id=1, source_target_pairs={{4,0},{8,4},{12,8},{16,12},{20,16},{24,20},{28,24},{5,1},{9,5},{13... | collective-permute-start | bytes 196616 | tf_op jit(solution)/shard_map/ppermute | solution.py:12
  432.0 29.3 %collective-permute-start = (bf16[128,256]{0,1:T(8,128)(2,1)S(1)}, bf16[128,256]{0,1:T(8,128)(2,1)S(1)}, u32[]{:S(2)}, u32[]{:S(2)}) collective-permute-start(bf16[128,256]{0,1:T(8,128)(2,1)S(1)} %bitcast.179), channel_id=1, source_target_pairs={{4,0},{8,4},{12,8},{16,12},{20,16},{24,20},{28,24},{5,1},{9,5},{13... | collective-permute-start | bytes 196616 | tf_op jit(solution)/shard_map/ppermute | solution.py:12
Sparse Core Ops, SparseCore 0:
  342.1 48.4 all-gather.3
  392.8 44.5 all-gather.5
where the time goes:
time: 472 us; the launch traced here: 469 us
  matrix products  133 us (28%)
  blocking collectives  86.1 us (18%)
  local copies, waits for them, and re-layouts  79.7 us (17%)
  starting transfers between devices  48.2 us (10%)
  other arithmetic  39.9 us (8%)
  waiting for transfers between devices  35.2 us (7%)
  loops' own time  31.3 us (7%)
  between operations  15.8 us (3%)
    all_gather x1, blocking collectives, shards(): lax.all_gather(beacon_values, 'ctx', axis=0, tiled=True)  33.4 us
    another operation x1, loops' own time, shards(): lax.map(per_head, jnp.arange(head_count, dtype=jnp.int32))  31.3 us
    all_gather x1, blocking collectives, shards(): lax.all_gather(beacon_keys, 'ctx', axis=0, tiled=True)  30.9 us
    dot_general x8, matrix products, head_grads(): jnp.dot(prob_half.T, grad_rows, preferred_element_type=jnp.float32)  29.9 us
    dot_general x8, matrix products, head_grads(): jnp.dot(grad_rows, value_rows.T, preferred_element_type=jnp.float32)  25.8 us
    dot_general x8, matrix products, head_grads(): jnp.dot(dscores.T, query_rows, preferred_element_type=jnp.float32)  23 us
    unnamed x1, blocking collectives  21.8 us
    dot_general x8, matrix products, head_grads(): jnp.dot(prob_half, value_rows, preferred_element_type=jnp.float32)  21.6 us
  transfers between devices with their start and end apart: 12, of which 5 were waited for; matrix products, arithmetic and copies ran while one was open for 17% of the time, Pallas kernels for 0%

commit v1 on v0

v1 whole, which is shorter than its diff:
```python
import functools
import math

import jax
import jax.numpy as jnp
from jax import lax
from jax.experimental import pallas as pl
from jax.experimental.pallas import tpu as pltpu
from jax.sharding import PartitionSpec as P

HD = 128
CORES = 2
BF = jnp.bfloat16
F32 = jnp.float32


def nt(a, b):
    return lax.dot_general(a, b, (((1,), (1,)), ((), ())), preferred_element_type=F32)


def nn(a, b):
    return jnp.dot(a, b, preferred_element_type=F32)


def attention_kernel(
    group, prev_groups, slots, half,
    count_ref, hi_ref,
    q_ref, g_ref, k_ref, v_ref, kp_ref, vp_ref, kb_ref, vb_ref,
    out_ref, gq_ref, dko_ref, dvo_ref, dkp_ref, dvp_ref, dkb_ref, dvb_ref,
    acc_k, acc_v,
):
    step = pl.program_id(1)
    rows = q_ref.shape[0]
    own = k_ref.shape[0]
    prev = kp_ref.shape[0]
    beac = kb_ref.shape[0]
    chunk = prev // prev_groups
    block = beac // slots
    scale = HD ** (-0.5)
    c = scale * math.log2(math.e)
    q = q_ref[...]
    g = g_ref[...]
    hi = hi_ref[0]
    count = count_ref[0]

    diag = lax.broadcasted_iota(jnp.int32, (half, half), 0) <= lax.broadcasted_iota(
        jnp.int32, (half, half), 1
    )
    pieces = []
    for i in range(0, own, half):
        pieces.append((i, i, k_ref[i : i + half, :], v_ref[i : i + half, :], None))
    for d in range(prev_groups):
        at = d * chunk
        pieces.append(
            (own + at, 0, kp_ref[at : at + chunk, :], vp_ref[at : at + chunk, :], hi > d)
        )
    for j in range(slots):
        at = j * block
        pieces.append(
            (own + prev + at, 0, kb_ref[at : at + block, :], vb_ref[at : at + block, :], count > j)
        )

    def pad_rows(x, start, fill):
        if start == 0:
            return x
        return jnp.concatenate([jnp.full((x.shape[0], start), fill, x.dtype), x], axis=1)

    scores = []
    row_max = None
    for _, start, keys, _, ok in pieces:
        s = nt(keys, q[start:, :])
        if ok is None:
            d = jnp.where(diag, s[:, :half], -1e30)
            s = d if s.shape[1] == half else jnp.concatenate([d, s[:, half:]], axis=1)
            top = jnp.max(s, axis=0, keepdims=True)
        else:
            top = jnp.max(s, axis=0, keepdims=True) + jnp.where(ok, 0.0, -1e30)
        top = pad_rows(top, start, -1e30)
        row_max = top if row_max is None else jnp.maximum(row_max, top)
        scores.append(s)
    shift = row_max * c
    weights = []
    total = None
    for (_, start, _, _, ok), s in zip(pieces, scores):
        m = shift[:, start:]
        if ok is not None:
            m = m + jnp.where(ok, 0.0, 1e30)
        w = jnp.exp2(s * c - m)
        part = pad_rows(jnp.sum(w, axis=0, keepdims=True), start, 0.0)
        total = part if total is None else total + part
        weights.append(w)
    inv = 1.0 / total
    out_t = None
    probs = []
    for (_, start, _, vals, _), w in zip(pieces, weights):
        p = (w * inv[:, start:]).astype(BF)
        probs.append(p)
        o = pad_rows(nn(vals.T, p), start, 0.0)
        out_t = o if out_t is None else out_t + o
    out = out_t.T.astype(BF)
    out_ref[...] = out
    delta = jnp.sum(out.astype(F32) * g.astype(F32), axis=1, keepdims=True).T
    r2 = inv * scale

    @pl.when(step == 0)
    def _():
        acc_k[...] = jnp.zeros_like(acc_k)
        acc_v[...] = jnp.zeros_like(acc_v)

    gq_t = None
    for (at, start, keys, vals, _), w, p in zip(pieces, weights, probs):
        n = keys.shape[0]
        dp = nt(vals, g[start:, :])
        ds = ((w * r2[:, start:]) * (dp - delta[:, start:])).astype(BF)
        acc_v[at : at + n, :] += nn(p, g[start:, :])
        acc_k[at : at + n, :] += nn(ds, q[start:, :])
        d = pad_rows(nn(keys.T, ds), start, 0.0)
        gq_t = d if gq_t is None else gq_t + d
    gq_ref[...] = gq_t.T.astype(BF)

    @pl.when(step == group - 1)
    def _():
        dko_ref[...] = acc_k[:own, :]
        dvo_ref[...] = acc_v[:own, :]
        dkp_ref[...] = acc_k[own : own + prev, :].astype(BF)
        dvp_ref[...] = acc_v[own : own + prev, :].astype(BF)
        dkb_ref[...] = acc_k[own + prev :, :].astype(BF)
        dvb_ref[...] = acc_v[own + prev :, :].astype(BF)


def attention(q, g, k, v, kp, vp, kb, vb, count, hi, prev_groups, slots):
    rows, q_cols = q.shape
    own, kv_cols = k.shape
    prev, beac = kp.shape[0], kb.shape[0]
    heads, kv_heads = q_cols // HD, kv_cols // HD
    group = heads // kv_heads
    half = own // 2
    per_q = pl.BlockSpec((rows, HD), lambda a, b, *_: (0, a * group + b))

    def per_kv(n):
        return pl.BlockSpec((n, HD), lambda a, b, *_: (0, a))

    keys = own + prev + beac
    return pl.pallas_call(
        functools.partial(attention_kernel, group, prev_groups, slots, half),
        grid_spec=pltpu.PrefetchScalarGridSpec(
            num_scalar_prefetch=2,
            grid=(kv_heads, group),
            in_specs=[per_q, per_q, per_kv(own), per_kv(own), per_kv(prev), per_kv(prev), per_kv(beac), per_kv(beac)],
            out_specs=[per_q, per_q, per_kv(own), per_kv(own), per_kv(prev), per_kv(prev), per_kv(beac), per_kv(beac)],
            scratch_shapes=[pltpu.VMEM((keys, HD), F32), pltpu.VMEM((keys, HD), F32)],
        ),
        out_shape=[
            jax.ShapeDtypeStruct(q.shape, BF),
            jax.ShapeDtypeStruct(q.shape, BF),
            jax.ShapeDtypeStruct(k.shape, F32),
            jax.ShapeDtypeStruct(k.shape, F32),
            jax.ShapeDtypeStruct(kp.shape, BF),
            jax.ShapeDtypeStruct(kp.shape, BF),
            jax.ShapeDtypeStruct(kb.shape, BF),
            jax.ShapeDtypeStruct(kb.shape, BF),
        ],
        compiler_params=pltpu.CompilerParams(vmem_limit_bytes=50 * 1024 * 1024),
        cost_estimate=pl.CostEstimate(
            flops=12 * heads * rows * keys * HD, bytes_accessed=4 * q.size * 2, transcendentals=heads * rows * keys
        ),
    )(count, hi, q, g, k, v, kp, vp, kb, vb)


def shards(
    queries, keys_in, values_in, grad_output, beacon_keys, beacon_values, read_blocks, read_counts
):
    tp = lax.axis_size("tp")
    owners = lax.axis_size("ctx")
    groups = tp // CORES
    t = lax.axis_index("tp")
    hi, lo = t // CORES, t % CORES
    tokens = queries.shape[0]
    block_rows, bw = beacon_keys.shape
    slots = read_blocks.shape[1]
    row, count = read_blocks[0], read_counts[0]

    def column_half(x, which):
        w = x.shape[1] // tp
        parts = [
            lax.dynamic_slice_in_dim(x, (CORES * j + which) * w, w, axis=1) for j in range(groups)
        ]
        return jnp.concatenate(parts, axis=1)

    sibling = [(i, i ^ 1) for i in range(tp)]

    def by_rank(mine, theirs, axis):
        first = jnp.where(lo == 0, mine, theirs)
        second = jnp.where(lo == 0, theirs, mine)
        return jnp.concatenate([first, second], axis=axis)

    def swap_in(*arrays):
        widths = [a.shape[1] // CORES for a in arrays]
        send = jnp.concatenate([column_half(a, 1 - lo) for a in arrays], axis=1)
        got = lax.ppermute(send, "tp", sibling)
        res, at = [], 0
        for a, w in zip(arrays, widths):
            res.append(by_rank(column_half(a, lo), got[:, at : at + w], 0))
            at += w
        return res

    all_b = lax.all_gather(
        jnp.concatenate([beacon_keys, beacon_values], axis=1), "ctx", axis=0, tiled=True
    )
    k, v = swap_in(keys_in, values_in)
    kv = jnp.concatenate([k, v], axis=1)
    prevs = []
    for d in range(1, groups):
        pairs = [(i, i + CORES * d) for i in range(tp - CORES * d)]
        prevs.append(lax.ppermute(kv, "tp", pairs))
    kvp = jnp.concatenate(prevs, axis=0)
    half_cols = k.shape[1]
    q, g = swap_in(queries, grad_output)

    mine = jnp.concatenate(
        [lax.dynamic_slice_in_dim(all_b, row[j] * block_rows, block_rows, axis=0) for j in range(slots)],
        axis=0,
    )
    quarters = [mine]
    for d in range(1, groups):
        pairs = [(i, (i + CORES * d) % tp) for i in range(tp)]
        quarters.append(lax.ppermute(mine, "tp", pairs))
    def ordered(lo_col, hi_col):
        res = []
        for j in range(groups):
            x = quarters[0][:, lo_col:hi_col]
            for d in range(1, groups):
                x = jnp.where((hi - d) % groups == j, quarters[d][:, lo_col:hi_col], x)
            res.append(x)
        return jnp.concatenate(res, axis=1)

    kb, vb = ordered(0, bw), ordered(bw, 2 * bw)

    out, gq, dko, dvo, dkp, dvp, dkb, dvb = attention(
        q, g, k, v, kvp[:, :half_cols], kvp[:, half_cols:], kb, vb,
        count[None], hi[None].astype(jnp.int32), groups - 1, slots,
    )

    def quarter(x, j):
        return lax.dynamic_slice_in_dim(x, j * bw, bw, axis=1)

    def both(j):
        return jnp.concatenate([quarter(dkb, j), quarter(dvb, j)], axis=1)

    beacon = both(hi).astype(F32)
    for d in range(1, groups):
        pairs = [(i, (i + CORES * d) % tp) for i in range(tp)]
        beacon = beacon + lax.ppermute(both((hi + d) % groups), "tp", pairs).astype(F32)
    beacon = beacon.reshape(slots, block_rows, 2 * bw)
    used = jnp.arange(slots, dtype=jnp.int32) < count
    ids = jnp.arange(owners, dtype=jnp.int32)
    dense = jnp.zeros((owners, block_rows, 2 * bw), F32)
    for j in range(slots):
        hit = (ids == row[j]) & used[j]
        dense = dense + jnp.where(hit[:, None, None], beacon[j][None], 0.0)
    dense = dense.astype(BF).reshape(owners * block_rows, 2 * bw)
    own_b = lax.psum_scatter(dense, "ctx", scatter_dimension=0, tiled=True)

    rows_g = k.shape[0]
    kvg = jnp.concatenate([dko, dvo], axis=1)
    back = jnp.concatenate([dkp, dvp], axis=1)
    for d in range(1, groups):
        pairs = [(i + CORES * d, i) for i in range(tp - CORES * d)]
        kvg = kvg + lax.ppermute(back[(d - 1) * rows_g : d * rows_g], "tp", pairs).astype(F32)
    kvg = kvg.astype(BF)

    def swap_out(*arrays):
        send = jnp.concatenate(
            [lax.dynamic_slice_in_dim(a, (1 - lo) * tokens, tokens, axis=0) for a in arrays], axis=1
        )
        got = lax.ppermute(send, "tp", sibling)
        res, at = [], 0
        for a in arrays:
            n = a.shape[1]
            keep = lax.dynamic_slice_in_dim(a, lo * tokens, tokens, axis=0)
            new = got[:, at : at + n]
            at += n
            w = n // groups
            cols = []
            for j in range(groups):
                cols.append(by_rank(keep[:, j * w : (j + 1) * w], new[:, j * w : (j + 1) * w], 1))
            res.append(jnp.concatenate(cols, axis=1))
        return res

    tok_out, tok_gq = swap_out(out, gq)
    tok_gk, tok_gv = swap_out(kvg[:, :half_cols], kvg[:, half_cols:])
    return (tok_out, tok_gq, tok_gk, tok_gv, own_b[:, :bw], own_b[:, bw:])


def solution(mesh):
    tok = P(("ctx", "tp"), None)
    bea = P("ctx", "tp")
    return jax.shard_map(
        shards,
        mesh=mesh,
        in_specs=(tok, tok, tok, tok, bea, bea, P("ctx", None), P("ctx")),
        out_specs=(tok, tok, tok, tok, bea, bea),
        check_vma=False,
    )
```

time: 472 us -> 243 us (0.51)
  matrix products: 133 us -> 0 us
  blocking collectives: 86.1 us -> 0 us
  waiting for transfers between devices: 35.2 us -> 110 us
  local copies, waits for them, and re-layouts: 79.7 us -> 11.8 us
  Pallas kernels: 0 us -> 63.8 us
  starting transfers between devices: 48.2 us -> 5.24 us
  loops' own time: 31.3 us -> 0 us
  other arithmetic: 39.9 us -> 32.3 us
    dot_general x48 -> x0, matrix products: 133 us -> none  [the longest x8 29.9 us: head_grads(): jnp.dot(prob_half.T, grad_rows, preferred_element_type=jnp.float32)]
    all_gather x2 -> x0, blocking collectives: 64.3 us -> none  [the longest x1 33.4 us: shards(): lax.all_gather(beacon_values, 'ctx', axis=0, tiled=True)]
    pallas_call x0 -> x1, Pallas kernels: none -> 63.8 us  [attention(): pl.pallas_call(functools.partial(attention_kernel, group, prev_groups, sl...]
    reduce_scatter x0 -> x1, waiting for transfers between devices: none -> 56.5 us  [shards(): own_b = lax.psum_scatter(dense, 'ctx', scatter_dimension=0, tiled=True)]
    ppermute x2 -> x8, waiting for transfers between devices: 0.01 us -> 53.5 us  [the longest x1 21.7 us: shards(): lax.ppermute(back[(d - 1) * rows_g:d * rows_g], 'tp', pairs).astype(F32)]
    all_to_all x8 -> x0, starting transfers between devices: 39.3 us -> none  [the longest x1 6.08 us: shards(): lax.all_to_all(seg_out, 'tp', split_axis=0, concat_axis=1, tiled=True)]
    all_to_all x8 -> x0, waiting for transfers between devices: 34.5 us -> none  [the longest x1 18.1 us: shards(): lax.all_to_all(seg_out, 'tp', split_axis=0, concat_axis=1, tiled=True)]
    another operation x1 -> x0, loops' own time: 31.3 us -> none  [shards(): lax.map(per_head, jnp.arange(head_count, dtype=jnp.int32))]
  transfers between devices with their start and end apart: 12 -> 10, of which waited for: 5 -> 5; matrix products, arithmetic and copies ran while one was open for 17% -> 16% of each run, Pallas kernels for 0% -> 0%
where the time goes in v1:
time: 243 us; the launch traced here: 241 us
  waiting for transfers between devices  110 us (45%)
  Pallas kernels  63.8 us (26%)
  other arithmetic  32.3 us (13%)
  between operations  17.7 us (7%)
  local copies, waits for them, and re-layouts  11.8 us (5%)
  starting transfers between devices  5.24 us (2%)
    pallas_call x1, Pallas kernels, attention(): pl.pallas_call(functools.partial(attention_kernel, group, prev_groups, sl...  63.8 us
    reduce_scatter x1, waiting for transfers between devices, shards(): own_b = lax.psum_scatter(dense, 'ctx', scatter_dimension=0, tiled=True)  56.5 us
    ppermute x1, waiting for transfers between devices, shards(): lax.ppermute(back[(d - 1) * rows_g:d * rows_g], 'tp', pairs).astype(F32)  21.7 us
    ppermute x1, waiting for transfers between devices, shards(): prevs.append(lax.ppermute(kv, 'tp', pairs))  18.1 us
    select_n x4, other arithmetic, by_rank(): first = jnp.where(lo == 0, mine, theirs)  8.18 us
    ppermute x1, waiting for transfers between devices, shards(): lax.ppermute(both((hi + d) % groups), 'tp', pairs).astype(F32)  7.06 us
    ppermute x1, waiting for transfers between devices, shards(): quarters.append(lax.ppermute(mine, 'tp', pairs))  6.71 us
    dynamic_slice x2, local copies, waits for them, and re-layouts, column_half(): lax.dynamic_slice_in_dim(x, (CORES * j + which) * w, w, axis=1)  5.1 us
  transfers between devices with their start and end apart: 10, of which 5 were waited for; matrix products, arithmetic and copies ran while one was open for 16% of the time, Pallas kernels for 0%

profile of v1, /device:TPU:12, one launch (start us, length us, event | category | flops | bytes accessed | tf_op | source)
XLA Modules:
  0.0 240.8 jit_solution(5892177942761146942)
XLA Ops:
  7.2 1.7 pad_maximum_fusion.21
  9.0 2.0 constant_dynamic-slice_fusion.13
  11.0 0.9 pad_maximum_fusion.9
  11.9 3.1 %constant_dynamic-slice_fusion.21 = (bf16[256,1024]{1,0:T(8,128)(2,1)S(1)}, bf16[256,1024]{1,0:T(8,128)(2,1)S(1)}, bf16[256,1024]{1,0:T(8,128)(2,1)S(1)}, bf16[2...) fusion(bf16[256,4096]{1,0:T(8,128)(2,1)S(1)} %copy-done, ...), kind=kLoop, calls=%fused_computation.83 | loop fusion | bytes 8388624 | tf_op jit(solution)/shard_map/dynamic_slice | solution.py:186
  15.0 1.5 pad_maximum_fusion
  16.5 0.5 collective-permute-start
  17.6 0.6 fusion.9
  18.3 0.6 fusion.10
  18.9 1.2 broadcast_select_fusion.17
  20.1 1.1 maximum_maximum_fusion
  21.3 1.3 collective-permute-start.2
  22.6 1.2 compare_and_fusion
  26.5 1.3 compare_and_fusion.1
  27.7 1.2 compare_and_fusion.2
  28.9 1.3 compare_and_fusion.3
  30.2 0.1 broadcast_bitcast_fusion
  30.3 0.1 broadcast_bitcast_fusion.2
  30.4 18.1 %collective-permute-done.2 = bf16[512,1024]{1,0:T(8,128)(2,1)} collective-permute-done((bf16[512,1024]{1,0:T(8,128)(2,1)}, bf16[512,1024]{1,0:T(8,128)(2,1)}, u32[]{:S(2)}, u32[]{:S(2)}) %collective-permute-start.2) | collective-permute-done | bytes 1048608 | tf_op jit(solution)/shard_map/ppermute | solution.py:215
  48.5 2.1 fusion.7
  50.6 1.2 constant_dynamic-slice_fusion.11
  51.8 0.6 collective-permute-start.3
  52.4 2.6 %broadcast_select_fusion.1 = (bf16[256,2048]{1,0:T(8,128)(2,1)S(1)}, bf16[256,2048]{1,0:T(8,128)(2,1)S(1)}, bf16[256,2048]{1,0:T(8,128)(2,1)S(1)}, bf16[256,2048]{1,0:T(8,128)(2,1)S(1)}) fusion(pred[]{:T(512)S(6)} %eq.81, bf16[256,4096]{1,0:T(8,128)(2,1)} %collective-permute-done, bf16[256,1024]{1,0:T(8,128)(2,1)S(1)} %get-tuple-element.43, ...), kind=kLoop, calls=%fused_computation.22 | loop fusion | flops 6291456 | bytes 8388609 | tf_op jit(solution)/shard_map/jit(_where)/select_n | solution.py:193
  55.0 1.6 pad_maximum_fusion.2.g_ref
  56.6 1.6 pad_maximum_fusion.1.q_ref
  58.2 6.7 %collective-permute-done.3 = bf16[512,512]{1,0:T(8,128)(2,1)S(1)} collective-permute-done((bf16[512,512]{1,0:T(8,128)(2,1)S(1)}, bf16[512,512]{1,0:T(8,128)(2,1)S(1)}, u32[]{:S(2)}, u32[]{:S(2)}) %collective-permute-start.3) | collective-permute-done | bytes 524320 | tf_op jit(solution)/shard_map/ppermute | solution.py:227
  64.9 0.1 broadcast_select_fusion.14
  65.0 1.0 pad_maximum_fusion.13
  66.0 63.8 %shard_map.127 = (bf16[512,2048]{1,0:T(8,128)(2,1)}, bf16[512,2048]{1,0:T(8,128)(2,1)}, f32[512,512]{1,0:T(8,128)}, f32[512,512]{1,0:T(8,128)}, bf16[512,512]{1,...) custom-call(s32[1]{0:T(128)} %copy.14.count_ref, ...), custom_call_target="tpu_custom_call" | custom-call | flops 19327352832 | bytes 8388608 | tf_op jit(solution)/shard_map/pallas_call | solution.py:144
  129.9 0.1 pad_maximum_fusion.8
  130.0 2.7 %collective-permute-start.5 = (bf16[512,1024]{1,0:T(8,128)(2,1)S(1)}, bf16[512,1024]{1,0:T(8,128)(2,1)S(1)}, u32[]{:S(2)}, u32[]{:S(2)}) collective-permute-start(bf16[512,1024]{1,0:T(8,128)(2,1)S(1)} %pad_maximum_fusion.8), channel_id=1, source_target_pairs={{2,0},{3,1},{6,4},{7,5},{10,8},{11,9},{14,12},{15,13},{18,16},{19,... | collective-permute-start | bytes 3145736 | tf_op jit(solution)/shard_map/ppermute | solution.py:269
  132.8 0.1 collective-permute-start.7
  132.9 0.1 constant_dynamic-slice_fusion.7
  133.0 0.1 constant_dynamic-slice_fusion.6
  133.1 1.5 pad_maximum_fusion.3
  134.6 21.7 %collective-permute-done.5 = bf16[512,1024]{1,0:T(8,128)(2,1)S(1)} collective-permute-done((bf16[512,1024]{1,0:T(8,128)(2,1)S(1)}, bf16[512,1024]{1,0:T(8,128)(2,1)S(1)}, u32[]{:S(2)}, u32[]{:S(2)}) %collective-permute-start.5) | collective-permute-done | bytes 1048608 | tf_op jit(solution)/shard_map/ppermute | solution.py:269
  156.3 0.3 fusion
  156.8 0.9 pad_maximum_fusion.15
  157.7 7.1 %collective-permute-done.7 = bf16[512,512]{1,0:T(8,128)(2,1)S(1)} collective-permute-done((bf16[512,512]{1,0:T(8,128)(2,1)S(1)}, bf16[512,512]{1,0:T(8,128)(2,1)S(1)}, u32[]{:S(2)}, u32[]{:S(2)}) %collective-permute-start.7) | collective-permute-done | bytes 524320 | tf_op jit(solution)/shard_map/ppermute | solution.py:253
  164.7 0.2 convert_add_fusion
  165.0 1.9 fusion.2
  166.9 1.5 broadcast_select_fusion.23
  168.4 0.9 pad_maximum_fusion.17
  169.3 0.9 pad_maximum_fusion.16
  170.1 2.9 %broadcast_select_fusion.7 = (bf16[256,1024]{1,0:T(8,128)(2,1)S(1)}, bf16[256,1024]{1,0:T(8,128)(2,1)S(1)}, bf16[256,1024]{1,0:T(8,128)(2,1)S(1)}, bf16[256,1024...) fusion(pred[]{:T(512)S(6)} %eq.81, ...), kind=kLoop, calls=%fused_computation.38 | loop fusion | flops 2097152 | bytes 8388617 | tf_op jit(solution)/shard_map/jit(_where)/select_n | solution.py:193
  173.0 1.5 pad_maximum_fusion.5
  174.5 1.5 pad_maximum_fusion.4
  176.0 56.5 %reduce-scatter.2.cloned.1.call-done = bf16[128,512]{1,0:T(8,128)(2,1)} async-done(((bf16[1024,512]{1,0:T(8,128)(2,1)}), bf16[128,512]{1,0:T(8,128)(2,1)}) %reduce-scatter.2.cloned.1.call-update) | async-done | bytes 131088 | tf_op jit(solution)/shard_map/reduce_scatter | solution.py:262
  232.5 1.5 fusion.8
  (43 shorter events, 0.6 us)
Async XLA Ops:
  7.2 4.7 %copy-start = (bf16[256,4096]{1,0:T(8,128)(2,1)S(1)}, bf16[256,4096]{1,0:T(8,128)(2,1)}, u32[]{:S(2)}) copy-start(bf16[256,4096]{1,0:T(8,128)(2,1)} %param.11) | copy-start | bytes 6291460
  7.2 43.4 %all-gather.2.cloned.1.call-start = ((), (), s32[]{:S(2)}) async-start(), calls=%async_computation.1 | async-start | bytes 1179648 | tf_op jit(solution)/shard_map/all_gather | solution.py:207
  8.9 223.6 %reduce-scatter.2.cloned.1.call-start = ((), (), s32[]{:S(2)}) async-start(), calls=%async_computation.2 | async-start | bytes 1179648 | tf_op jit(solution)/shard_map/reduce_scatter | solution.py:262
  11.9 7.0 %collective-permute-start.1 = (bf16[256,1024]{1,0:T(8,128)(2,1)}, bf16[256,1024]{1,0:T(8,128)(2,1)}, u32[]{:S(2)}, u32[]{:S(2)}) collective-permute-start(bf16[256,1024]{1,0:T(8,128)(2,1)} %pad_maximum_fusion.9), channel_id=1, source_target_pairs={{0,1},{1,0},{2,3},{3,2},{4,5},{5,4},{6,7},{7,6},{8,9},{9,8},{10,11... | collective-permute-start | bytes 1572872 | tf_op jit(solution)/shard_map/ppermute | solution.py:200
  15.0 3.3 %copy-start.9 = (s32[1,4]{1,0:T(1,128)S(1)}, s32[1,4]{1,0:T(1,128)}, u32[]{:S(2)}) copy-start(s32[1,4]{1,0:T(1,128)} %param.14) | copy-start | bytes 52
  15.0 3.9 %copy-start.8 = (bf16[256,256]{1,0:T(8,128)(2,1)S(1)}, bf16[256,256]{1,0:T(8,128)(2,1)}, u32[]{:S(2)}) copy-start(bf16[256,256]{1,0:T(8,128)(2,1)} %get-tuple-element.111) | copy-start | bytes 393220
  16.5 35.9 %collective-permute-start = (bf16[256,4096]{1,0:T(8,128)(2,1)}, bf16[256,4096]{1,0:T(8,128)(2,1)}, u32[]{:S(2)}, u32[]{:S(2)}) collective-permute-start(bf16[256,4096]{1,0:T(8,128)(2,1)} %pad_maximum_fusion), channel_id=1, source_target_pairs={{0,1},{1,0},{2,3},{3,2},{4,5},{5,4},{6,7},{7,6},{8,9},{9,8},{10,11... | collective-permute-start | bytes 6291464 | tf_op jit(solution)/shard_map/ppermute | solution.py:200
  21.3 27.3 %collective-permute-start.2 = (bf16[512,1024]{1,0:T(8,128)(2,1)}, bf16[512,1024]{1,0:T(8,128)(2,1)}, u32[]{:S(2)}, u32[]{:S(2)}) collective-permute-start(bf16[512,1024]{1,0:T(8,128)(2,1)} %maximum_maximum_fusion), channel_id=1, source_target_pairs={{0,2},{1,3},{4,6},{5,7},{8,10},{9,11},{12,14},{13,15},{16,18},{17,... | collective-permute-start | bytes 3145736 | tf_op jit(solution)/shard_map/ppermute | solution.py:215
  30.4 22.0 %copy-start.4 = (bf16[256,1024]{1,0:T(8,128)(2,1)S(1)}, bf16[256,1024]{1,0:T(8,128)(2,1)}, u32[]{:S(2)}) copy-start(bf16[256,1024]{1,0:T(8,128)(2,1)} %get-tuple-element.106) | copy-start | bytes 1572868
  50.6 1.8 copy-start.5
  51.8 13.0 %collective-permute-start.3 = (bf16[512,512]{1,0:T(8,128)(2,1)S(1)}, bf16[512,512]{1,0:T(8,128)(2,1)S(1)}, u32[]{:S(2)}, u32[]{:S(2)}) collective-permute-start(bf16[512,512]{1,0:T(8,128)(2,1)S(1)} %pad_maximum_fusion.12), channel_id=1, source_target_pairs={{0,2},{1,3},{2,0},{3,1},{4,6},{5,7},{6,4},{7,5},{8,10},{9,11},{10,... | collective-permute-start | bytes 1572872 | tf_op jit(solution)/shard_map/ppermute | solution.py:227
  129.8 3.1 %copy-start.1 = (bf16[512,2048]{1,0:T(8,128)(2,1)S(1)}, bf16[512,2048]{1,0:T(8,128)(2,1)}, u32[]{:S(2)}) copy-start(bf16[512,2048]{1,0:T(8,128)(2,1)} %get-tuple-element.14) | copy-start | bytes 6291460
  130.0 3.0 %copy-start.2 = (bf16[512,2048]{1,0:T(8,128)(2,1)S(1)}, bf16[512,2048]{1,0:T(8,128)(2,1)}, u32[]{:S(2)}) copy-start(bf16[512,2048]{1,0:T(8,128)(2,1)} %get-tuple-element.15) | copy-start | bytes 6291460
  130.0 26.3 %collective-permute-start.5 = (bf16[512,1024]{1,0:T(8,128)(2,1)S(1)}, bf16[512,1024]{1,0:T(8,128)(2,1)S(1)}, u32[]{:S(2)}, u32[]{:S(2)}) collective-permute-start(bf16[512,1024]{1,0:T(8,128)(2,1)S(1)} %pad_maximum_fusion.8), channel_id=1, source_target_pairs={{2,0},{3,1},{6,4},{7,5},{10,8},{11,9},{14,12},{15,13},{18,16},{19,... | collective-permute-start | bytes 3145736 | tf_op jit(solution)/shard_map/ppermute | solution.py:269
  132.8 31.9 %collective-permute-start.7 = (bf16[512,512]{1,0:T(8,128)(2,1)S(1)}, bf16[512,512]{1,0:T(8,128)(2,1)S(1)}, u32[]{:S(2)}, u32[]{:S(2)}) collective-permute-start(bf16[512,512]{1,0:T(8,128)(2,1)S(1)} %pad_maximum_fusion.18), channel_id=1, source_target_pairs={{0,2},{1,3},{2,0},{3,1},{4,6},{5,7},{6,4},{7,5},{8,10},{9,11},{10,... | collective-permute-start | bytes 1572872 | tf_op jit(solution)/shard_map/ppermute | solution.py:253
  133.1 23.2 %copy-start.6 = (f32[512,512]{1,0:T(8,128)S(1)}, f32[512,512]{1,0:T(8,128)}, u32[]{:S(2)}) copy-start(f32[512,512]{1,0:T(8,128)} %get-tuple-element.16) | copy-start | bytes 3145732
  133.1 23.2 %copy-start.7 = (f32[512,512]{1,0:T(8,128)S(1)}, f32[512,512]{1,0:T(8,128)}, u32[]{:S(2)}) copy-start(f32[512,512]{1,0:T(8,128)} %get-tuple-element.17) | copy-start | bytes 3145732
  134.6 35.5 %collective-permute-start.4 = (bf16[256,4096]{1,0:T(8,128)(2,1)}, bf16[256,4096]{1,0:T(8,128)(2,1)}, u32[]{:S(2)}, u32[]{:S(2)}) collective-permute-start(bf16[256,4096]{1,0:T(8,128)(2,1)} %pad_maximum_fusion.3), channel_id=1, source_target_pairs={{0,1},{1,0},{2,3},{3,2},{4,5},{5,4},{6,7},{7,6},{8,9},{9,8},{10,11... | collective-permute-start | bytes 6291464 | tf_op jit(solution)/shard_map/ppermute | solution.py:276
  157.6 9.3 %collective-permute-start.6 = (bf16[256,1024]{1,0:T(8,128)(2,1)}, bf16[256,1024]{1,0:T(8,128)(2,1)}, u32[]{:S(2)}, u32[]{:S(2)}) collective-permute-start(bf16[256,1024]{1,0:T(8,128)(2,1)} %pad_maximum_fusion.15), channel_id=1, source_target_pairs={{0,1},{1,0},{2,3},{3,2},{4,5},{5,4},{6,7},{7,6},{8,9},{9,8},{10,11... | collective-permute-start | bytes 1572872 | tf_op jit(solution)/shard_map/ppermute | solution.py:276
  166.9 3.2 %copy-start.3 = (bf16[512,2048]{1,0:T(8,128)(2,1)S(1)}, bf16[512,2048]{1,0:T(8,128)(2,1)}, u32[]{:S(2)}) copy-start(bf16[512,2048]{1,0:T(8,128)(2,1)} %get-tuple-element.15) | copy-start | bytes 6291460
Sparse Core Ops, SparseCore 0:
  10.1 40.3 all-gather.1
  167.0 65.3 reduce-scatter.1

commit v2 on v1

--- a/solution.py
+++ b/solution.py
@@ -167,6 +167,69 @@
     )(count, hi, q, g, k, v, kp, vp, kb, vb)
 
 
+def owners_kernel(dense_ref, out_ref, got, total, send_sem, recv_sem):
+    me = lax.axis_index("ctx")
+    n = got.shape[0]
+    block = got.shape[1]
+    barrier = pltpu.get_barrier_semaphore()
+    for d in range(1, n):
+        pl.semaphore_signal(
+            barrier, inc=1, device_id={"ctx": lax.rem(me + d, n)}, device_id_type=pl.DeviceIdType.MESH
+        )
+    pl.semaphore_wait(barrier, n - 1)
+
+    def copy(d):
+        to = jnp.maximum(me - d, 0)
+        return pltpu.make_async_remote_copy(
+            src_ref=dense_ref.at[pl.ds(pl.multiple_of(to * block, block), block)],
+            dst_ref=got.at[d],
+            send_sem=send_sem.at[d],
+            recv_sem=recv_sem.at[d],
+            device_id={"ctx": to},
+            device_id_type=pl.DeviceIdType.MESH,
+        )
+
+    for d in range(n - 1, 0, -1):
+
+        @pl.when(me >= d)
+        def _(d=d):
+            copy(d).start()
+
+    total[...] = jnp.zeros_like(total)
+    for d in range(1, n):
+
+        @pl.when(me + d < n)
+        def _(d=d):
+            copy(d).wait_recv()
+            total[...] += got[d].astype(F32)
+
+    out_ref[...] = total[...].astype(BF)
+    for d in range(1, n):
+
+        @pl.when(me >= d)
+        def _(d=d):
+            copy(d).wait_send()
+
+
+def to_owners(dense, owners):
+    block, width = dense.shape[0] // owners, dense.shape[1]
+    return pl.pallas_call(
+        owners_kernel,
+        out_shape=jax.ShapeDtypeStruct((block, width), BF),
+        in_specs=[pl.BlockSpec(memory_space=pltpu.VMEM)],
+        out_specs=pl.BlockSpec(memory_space=pltpu.VMEM),
+        scratch_shapes=[
+            pltpu.VMEM((owners, block, width), BF),
+            pltpu.VMEM((block, width), F32),
+            pltpu.SemaphoreType.DMA((owners,)),
+            pltpu.SemaphoreType.DMA((owners,)),
+        ],
+        compiler_params=pltpu.CompilerParams(
+            collective_id=1, has_side_effects=True, vmem_limit_bytes=32 * 1024 * 1024
+        ),
+    )(dense)
+
+
 def shards(
     queries, keys_in, values_in, grad_output, beacon_keys, beacon_values, read_blocks, read_counts
 ):
@@ -259,7 +322,7 @@
         hit = (ids == row[j]) & used[j]
         dense = dense + jnp.where(hit[:, None, None], beacon[j][None], 0.0)
     dense = dense.astype(BF).reshape(owners * block_rows, 2 * bw)
-    own_b = lax.psum_scatter(dense, "ctx", scatter_dimension=0, tiled=True)
+    own_b = to_owners(dense, owners)
 
     rows_g = k.shape[0]
     kvg = jnp.concatenate([dko, dvo], axis=1)

time: 243 us -> 208 us (0.86)
  the two profiles are of different devices: /device:TPU:12 before, /device:TPU:11 now
where the time goes in v2:
time: 208 us; the launch traced here: 207 us
  Pallas kernels  91.3 us (44%)
  waiting for transfers between devices  41.8 us (20%)
  other arithmetic  26.5 us (13%)
  starting transfers between devices  19.1 us (9%)
  between operations  17.5 us (8%)
  local copies, waits for them, and re-layouts  11 us (5%)
    pallas_call x1, Pallas kernels, attention(): pl.pallas_call(functools.partial(attention_kernel, group, prev_groups, sl...  63.7 us
    pallas_call x1, Pallas kernels, to_owners(): pl.pallas_call(owners_kernel, out_shape=jax.ShapeDtypeStruct((block, widt...  27.6 us
    ppermute x1, waiting for transfers between devices, shards(): lax.ppermute(back[(d - 1) * rows_g:d * rows_g], 'tp', pairs).astype(F32)  17.9 us
    ppermute x1, waiting for transfers between devices, shards(): prevs.append(lax.ppermute(kv, 'tp', pairs))  13.7 us
    ppermute x2, starting transfers between devices, swap_out(): got = lax.ppermute(send, 'tp', sibling)  8.17 us
    select_n x4, other arithmetic, by_rank(): first = jnp.where(lo == 0, mine, theirs)  5.36 us
    ppermute x1, waiting for transfers between devices, shards(): lax.ppermute(both((hi + d) % groups), 'tp', pairs).astype(F32)  5.13 us
    ppermute x1, waiting for transfers between devices, shards(): quarters.append(lax.ppermute(mine, 'tp', pairs))  5.1 us
  transfers between devices with their start and end apart: 9, of which 4 were waited for; matrix products, arithmetic and copies ran while one was open for 15% of the time, Pallas kernels for 13%

profile of v2, /device:TPU:11, one launch (start us, length us, event | category | flops | bytes accessed | tf_op | source)
XLA Modules:
  0.0 207.2 jit_solution(247066498050241755)
XLA Ops:
  7.2 1.7 pad_maximum_fusion.21
  8.9 2.0 constant_dynamic-slice_fusion.13
  11.0 0.9 pad_maximum_fusion.9
  11.8 0.7 collective-permute-start.1
  12.5 3.1 %constant_dynamic-slice_fusion.21 = (bf16[256,1024]{1,0:T(8,128)(2,1)S(1)}, bf16[256,1024]{1,0:T(8,128)(2,1)S(1)}, bf16[256,1024]{1,0:T(8,128)(2,1)S(1)}, bf16[2...) fusion(bf16[256,4096]{1,0:T(8,128)(2,1)S(1)} %copy-done, ...), kind=kLoop, calls=%fused_computation.83 | loop fusion | bytes 8388624 | tf_op jit(solution)/shard_map/dynamic_slice | solution.py:249
  15.6 1.5 pad_maximum_fusion
  17.8 0.7 fusion.9
  18.4 0.6 fusion.10
  19.1 1.2 broadcast_select_fusion.17
  20.3 1.1 maximum_maximum_fusion
  21.4 4.1 %collective-permute-start.2 = (bf16[512,1024]{1,0:T(8,128)(2,1)}, bf16[512,1024]{1,0:T(8,128)(2,1)}, u32[]{:S(2)}, u32[]{:S(2)}) collective-permute-start(bf16[512,1024]{1,0:T(8,128)(2,1)} %maximum_maximum_fusion), channel_id=1, source_target_pairs={{0,2},{1,3},{4,6},{5,7},{8,10},{9,11},{12,14},{13,15},{16,18},{17,... | collective-permute-start | bytes 3145736 | tf_op jit(solution)/shard_map/ppermute | solution.py:278
  25.6 1.2 compare_and_fusion
  29.3 1.3 compare_and_fusion.1
  30.6 1.2 compare_and_fusion.2
  31.8 1.2 compare_and_fusion.3
  33.0 0.1 broadcast_bitcast_fusion
  33.0 0.1 broadcast_bitcast_fusion.2
  33.2 13.7 %collective-permute-done.2 = bf16[512,1024]{1,0:T(8,128)(2,1)} collective-permute-done((bf16[512,1024]{1,0:T(8,128)(2,1)}, bf16[512,1024]{1,0:T(8,128)(2,1)}, u32[]{:S(2)}, u32[]{:S(2)}) %collective-permute-start.2) | collective-permute-done | bytes 1048608 | tf_op jit(solution)/shard_map/ppermute | solution.py:278
  46.9 2.1 fusion.7
  49.0 1.2 constant_dynamic-slice_fusion.11
  50.2 2.3 %collective-permute-start.3 = (bf16[512,512]{1,0:T(8,128)(2,1)S(1)}, bf16[512,512]{1,0:T(8,128)(2,1)S(1)}, u32[]{:S(2)}, u32[]{:S(2)}) collective-permute-start(bf16[512,512]{1,0:T(8,128)(2,1)S(1)} %pad_maximum_fusion.12), channel_id=1, source_target_pairs={{0,2},{1,3},{2,0},{3,1},{4,6},{5,7},{6,4},{7,5},{8,10},{9,11},{10,... | collective-permute-start | bytes 1572872 | tf_op jit(solution)/shard_map/ppermute | solution.py:290
  52.5 2.6 %broadcast_select_fusion.1 = (bf16[256,2048]{1,0:T(8,128)(2,1)S(1)}, bf16[256,2048]{1,0:T(8,128)(2,1)S(1)}, bf16[256,2048]{1,0:T(8,128)(2,1)S(1)}, bf16[256,2048]{1,0:T(8,128)(2,1)S(1)}) fusion(pred[]{:T(512)S(6)} %eq.81, bf16[256,4096]{1,0:T(8,128)(2,1)} %collective-permute-done, bf16[256,1024]{1,0:T(8,128)(2,1)S(1)} %get-tuple-element.43, ...), kind=kLoop, calls=%fused_computation.22 | loop fusion | flops 6291456 | bytes 8388609 | tf_op jit(solution)/shard_map/jit(_where)/select_n | solution.py:256
  55.1 1.6 pad_maximum_fusion.2.g_ref
  56.7 1.6 pad_maximum_fusion.1.q_ref
  58.2 5.1 %collective-permute-done.3 = bf16[512,512]{1,0:T(8,128)(2,1)S(1)} collective-permute-done((bf16[512,512]{1,0:T(8,128)(2,1)S(1)}, bf16[512,512]{1,0:T(8,128)(2,1)S(1)}, u32[]{:S(2)}, u32[]{:S(2)}) %collective-permute-start.3) | collective-permute-done | bytes 524320 | tf_op jit(solution)/shard_map/ppermute | solution.py:290
  63.4 1.0 pad_maximum_fusion.13
  64.5 63.7 %shard_map.127 = (bf16[512,2048]{1,0:T(8,128)(2,1)}, bf16[512,2048]{1,0:T(8,128)(2,1)}, f32[512,512]{1,0:T(8,128)}, f32[512,512]{1,0:T(8,128)}, bf16[512,512]{1,...) custom-call(s32[1]{0:T(128)} %copy.14.count_ref, ...), custom_call_target="tpu_custom_call" | custom-call | flops 19327352832 | bytes 8388608 | tf_op jit(solution)/shard_map/pallas_call | solution.py:144
  128.3 0.1 pad_maximum_fusion.8
  128.4 1.6 collective-permute-start.5
  130.0 2.2 %collective-permute-start.7 = (bf16[512,512]{1,0:T(8,128)(2,1)S(1)}, bf16[512,512]{1,0:T(8,128)(2,1)S(1)}, u32[]{:S(2)}, u32[]{:S(2)}) collective-permute-start(bf16[512,512]{1,0:T(8,128)(2,1)S(1)} %pad_maximum_fusion.18), channel_id=1, source_target_pairs={{0,2},{1,3},{2,0},{3,1},{4,6},{5,7},{6,4},{7,5},{8,10},{9,11},{10,... | collective-permute-start | bytes 1572872 | tf_op jit(solution)/shard_map/ppermute | solution.py:316
  132.3 0.1 constant_dynamic-slice_fusion.7
  132.4 0.1 constant_dynamic-slice_fusion.6
  132.5 0.2 pad_maximum_fusion.3
  132.7 2.6 %collective-permute-start.4 = (bf16[256,4096]{1,0:T(8,128)(2,1)S(1)}, bf16[256,4096]{1,0:T(8,128)(2,1)S(1)}, u32[]{:S(2)}, u32[]{:S(2)}) collective-permute-start(bf16[256,4096]{1,0:T(8,128)(2,1)S(1)} %pad_maximum_fusion.3), channel_id=1, source_target_pairs={{0,1},{1,0},{2,3},{3,2},{4,5},{5,4},{6,7},{7,6},{8,9},{9,8},{10,11... | collective-permute-start | bytes 6291464 | tf_op jit(solution)/shard_map/ppermute | solution.py:339
  135.4 17.9 %collective-permute-done.5 = bf16[512,1024]{1,0:T(8,128)(2,1)S(1)} collective-permute-done((bf16[512,1024]{1,0:T(8,128)(2,1)S(1)}, bf16[512,1024]{1,0:T(8,128)(2,1)S(1)}, u32[]{:S(2)}, u32[]{:S(2)}) %collective-permute-start.5) | collective-permute-done | bytes 1048608 | tf_op jit(solution)/shard_map/ppermute | solution.py:332
  153.2 0.3 fusion
  153.8 5.5 %collective-permute-start.6 = (bf16[256,1024]{1,0:T(8,128)(2,1)S(1)}, bf16[256,1024]{1,0:T(8,128)(2,1)S(1)}, u32[]{:S(2)}, u32[]{:S(2)}) collective-permute-start(bf16[256,1024]{1,0:T(8,128)(2,1)S(1)} %pad_maximum_fusion.15), channel_id=1, source_target_pairs={{0,1},{1,0},{2,3},{3,2},{4,5},{5,4},{6,7},{7,6},{8,9},{9,8},{10,11... | collective-permute-start | bytes 1572872 | tf_op jit(solution)/shard_map/ppermute | solution.py:339
  159.3 5.1 %collective-permute-done.7 = bf16[512,512]{1,0:T(8,128)(2,1)S(1)} collective-permute-done((bf16[512,512]{1,0:T(8,128)(2,1)S(1)}, bf16[512,512]{1,0:T(8,128)(2,1)S(1)}, u32[]{:S(2)}, u32[]{:S(2)}) %collective-permute-start.7) | collective-permute-done | bytes 524320 | tf_op jit(solution)/shard_map/ppermute | solution.py:316
  164.5 0.2 convert_add_fusion
  164.7 1.1 fusion.2.dense_ref
  165.8 27.6 %shard_map.128 = bf16[128,512]{1,0:T(8,128)(2,1)S(1)} custom-call(bf16[1024,512]{1,0:T(8,128)(2,1)S(1)} %fusion.2.dense_ref), custom_call_target="tpu_custom_call" | custom-call | tf_op jit(solution)/shard_map/pallas_call | solution.py:216
  193.4 0.7 fusion.8
  194.1 0.2 broadcast_select_fusion.23
  194.3 0.9 pad_maximum_fusion.17
  195.2 0.9 pad_maximum_fusion.16
  196.1 1.3 broadcast_select_fusion.7
  197.4 1.5 pad_maximum_fusion.5
  198.8 1.5 pad_maximum_fusion.4
  (39 shorter events, 0.7 us)
Async XLA Ops:
  7.2 5.3 %copy-start = (bf16[256,4096]{1,0:T(8,128)(2,1)S(1)}, bf16[256,4096]{1,0:T(8,128)(2,1)}, u32[]{:S(2)}) copy-start(bf16[256,4096]{1,0:T(8,128)(2,1)} %param.11) | copy-start | bytes 6291460
  7.2 41.8 %all-gather.2.cloned.1.call-start = ((), (), s32[]{:S(2)}) async-start(), calls=%async_computation | async-start | bytes 1179648 | tf_op jit(solution)/shard_map/all_gather | solution.py:270
  11.8 7.3 %collective-permute-start.1 = (bf16[256,1024]{1,0:T(8,128)(2,1)}, bf16[256,1024]{1,0:T(8,128)(2,1)}, u32[]{:S(2)}, u32[]{:S(2)}) collective-permute-start(bf16[256,1024]{1,0:T(8,128)(2,1)} %pad_maximum_fusion.9), channel_id=1, source_target_pairs={{0,1},{1,0},{2,3},{3,2},{4,5},{5,4},{6,7},{7,6},{8,9},{9,8},{10,11... | collective-permute-start | bytes 1572872 | tf_op jit(solution)/shard_map/ppermute | solution.py:263
  15.6 2.8 %copy-start.8 = (s32[1,4]{1,0:T(1,128)S(1)}, s32[1,4]{1,0:T(1,128)}, u32[]{:S(2)}) copy-start(s32[1,4]{1,0:T(1,128)} %param.14) | copy-start | bytes 52
  15.6 3.5 %copy-start.7 = (bf16[256,256]{1,0:T(8,128)(2,1)S(1)}, bf16[256,256]{1,0:T(8,128)(2,1)}, u32[]{:S(2)}) copy-start(bf16[256,256]{1,0:T(8,128)(2,1)} %get-tuple-element.111) | copy-start | bytes 393220
  17.1 35.4 %collective-permute-start = (bf16[256,4096]{1,0:T(8,128)(2,1)}, bf16[256,4096]{1,0:T(8,128)(2,1)}, u32[]{:S(2)}, u32[]{:S(2)}) collective-permute-start(bf16[256,4096]{1,0:T(8,128)(2,1)} %pad_maximum_fusion), channel_id=1, source_target_pairs={{0,1},{1,0},{2,3},{3,2},{4,5},{5,4},{6,7},{7,6},{8,9},{9,8},{10,11... | collective-permute-start | bytes 6291464 | tf_op jit(solution)/shard_map/ppermute | solution.py:263
  21.4 25.5 %collective-permute-start.2 = (bf16[512,1024]{1,0:T(8,128)(2,1)}, bf16[512,1024]{1,0:T(8,128)(2,1)}, u32[]{:S(2)}, u32[]{:S(2)}) collective-permute-start(bf16[512,1024]{1,0:T(8,128)(2,1)} %maximum_maximum_fusion), channel_id=1, source_target_pairs={{0,2},{1,3},{4,6},{5,7},{8,10},{9,11},{12,14},{13,15},{16,18},{17,... | collective-permute-start | bytes 3145736 | tf_op jit(solution)/shard_map/ppermute | solution.py:278
  33.2 19.3 %copy-start.3 = (bf16[256,1024]{1,0:T(8,128)(2,1)S(1)}, bf16[256,1024]{1,0:T(8,128)(2,1)}, u32[]{:S(2)}) copy-start(bf16[256,1024]{1,0:T(8,128)(2,1)} %get-tuple-element.106) | copy-start | bytes 1572868
  49.0 3.5 %copy-start.4 = (bf16[256,1024]{1,0:T(8,128)(2,1)S(1)}, bf16[256,1024]{1,0:T(8,128)(2,1)}, u32[]{:S(2)}) copy-start(bf16[256,1024]{1,0:T(8,128)(2,1)} %get-tuple-element.107) | copy-start | bytes 1572868
  50.2 13.1 %collective-permute-start.3 = (bf16[512,512]{1,0:T(8,128)(2,1)S(1)}, bf16[512,512]{1,0:T(8,128)(2,1)S(1)}, u32[]{:S(2)}, u32[]{:S(2)}) collective-permute-start(bf16[512,512]{1,0:T(8,128)(2,1)S(1)} %pad_maximum_fusion.12), channel_id=1, source_target_pairs={{0,2},{1,3},{2,0},{3,1},{4,6},{5,7},{6,4},{7,5},{8,10},{9,11},{10,... | collective-permute-start | bytes 1572872 | tf_op jit(solution)/shard_map/ppermute | solution.py:290
  128.2 4.0 %copy-start.1 = (bf16[512,2048]{1,0:T(8,128)(2,1)S(1)}, bf16[512,2048]{1,0:T(8,128)(2,1)}, u32[]{:S(2)}) copy-start(bf16[512,2048]{1,0:T(8,128)(2,1)} %get-tuple-element.14) | copy-start | bytes 6291460
  128.4 3.9 %copy-start.2 = (bf16[512,2048]{1,0:T(8,128)(2,1)S(1)}, bf16[512,2048]{1,0:T(8,128)(2,1)}, u32[]{:S(2)}) copy-start(bf16[512,2048]{1,0:T(8,128)(2,1)} %get-tuple-element.15) | copy-start | bytes 6291460
  128.4 24.8 %collective-permute-start.5 = (bf16[512,1024]{1,0:T(8,128)(2,1)S(1)}, bf16[512,1024]{1,0:T(8,128)(2,1)S(1)}, u32[]{:S(2)}, u32[]{:S(2)}) collective-permute-start(bf16[512,1024]{1,0:T(8,128)(2,1)S(1)} %pad_maximum_fusion.8), channel_id=1, source_target_pairs={{2,0},{3,1},{6,4},{7,5},{10,8},{11,9},{14,12},{15,13},{18,16},{19,... | collective-permute-start | bytes 3145736 | tf_op jit(solution)/shard_map/ppermute | solution.py:332
  130.0 34.4 %collective-permute-start.7 = (bf16[512,512]{1,0:T(8,128)(2,1)S(1)}, bf16[512,512]{1,0:T(8,128)(2,1)S(1)}, u32[]{:S(2)}, u32[]{:S(2)}) collective-permute-start(bf16[512,512]{1,0:T(8,128)(2,1)S(1)} %pad_maximum_fusion.18), channel_id=1, source_target_pairs={{0,2},{1,3},{2,0},{3,1},{4,6},{5,7},{6,4},{7,5},{8,10},{9,11},{10,... | collective-permute-start | bytes 1572872 | tf_op jit(solution)/shard_map/ppermute | solution.py:316
  132.5 20.7 %copy-start.5 = (f32[512,512]{1,0:T(8,128)S(1)}, f32[512,512]{1,0:T(8,128)}, u32[]{:S(2)}) copy-start(f32[512,512]{1,0:T(8,128)} %get-tuple-element.16) | copy-start | bytes 3145732
  132.5 20.7 %copy-start.6 = (f32[512,512]{1,0:T(8,128)S(1)}, f32[512,512]{1,0:T(8,128)}, u32[]{:S(2)}) copy-start(f32[512,512]{1,0:T(8,128)} %get-tuple-element.17) | copy-start | bytes 3145732
  132.7 63.3 %collective-permute-start.4 = (bf16[256,4096]{1,0:T(8,128)(2,1)S(1)}, bf16[256,4096]{1,0:T(8,128)(2,1)S(1)}, u32[]{:S(2)}, u32[]{:S(2)}) collective-permute-start(bf16[256,4096]{1,0:T(8,128)(2,1)S(1)} %pad_maximum_fusion.3), channel_id=1, source_target_pairs={{0,1},{1,0},{2,3},{3,2},{4,5},{5,4},{6,7},{7,6},{8,9},{9,8},{10,11... | collective-permute-start | bytes 6291464 | tf_op jit(solution)/shard_map/ppermute | solution.py:339
  153.8 40.3 %collective-permute-start.6 = (bf16[256,1024]{1,0:T(8,128)(2,1)S(1)}, bf16[256,1024]{1,0:T(8,128)(2,1)S(1)}, u32[]{:S(2)}, u32[]{:S(2)}) collective-permute-start(bf16[256,1024]{1,0:T(8,128)(2,1)S(1)} %pad_maximum_fusion.15), channel_id=1, source_target_pairs={{0,1},{1,0},{2,3},{3,2},{4,5},{5,4},{6,7},{7,6},{8,9},{9,8},{10,11... | collective-permute-start | bytes 1572872 | tf_op jit(solution)/shard_map/ppermute | solution.py:339
Sparse Core Ops, SparseCore 0:
  10.1 38.7 all-gather.1

commit v3 on v1

--- a/solution.py
+++ b/solution.py
@@ -167,6 +167,193 @@
     )(count, hi, q, g, k, v, kp, vp, kb, vb)
 
 
+def deliver_kernel(
+    groups, owners, slots,
+    row_ref, count_ref, out_ref, gq_ref, dko_ref, dvo_ref, dkp_ref, dvp_ref, dkb_ref, dvb_ref,
+    tout_ref, tgq_ref, tgk_ref, tgv_ref, bk_ref, bv_ref,
+    near, back, summed, part, send, got,
+    near_s, near_r, back_s, back_r, tok_s, tok_r, tok_l, kv_s, kv_r, kv_l, own_s, own_r,
+):
+    mesh_id = pl.DeviceIdType.MESH
+    me = lax.axis_index("ctx")
+    t = lax.axis_index("tp")
+    hi, lo = t // CORES, t % CORES
+    other = 1 - lo
+    sibling = {"tp": hi * CORES + other}
+    rows = dko_ref.shape[0]
+    tokens = tout_ref.shape[0]
+    block, bw = bk_ref.shape
+
+    barrier = pltpu.get_barrier_semaphore()
+    pl.semaphore_signal(barrier, inc=1, device_id=sibling, device_id_type=mesh_id)
+    for d in range(1, groups):
+        pl.semaphore_signal(
+            barrier, inc=1, device_id={"tp": lax.rem(hi + d, groups) * CORES + lo}, device_id_type=mesh_id
+        )
+    for d in range(1, owners):
+        pl.semaphore_signal(
+            barrier, inc=1, device_id={"ctx": lax.rem(me + d, owners)}, device_id_type=mesh_id
+        )
+    pl.semaphore_wait(barrier, 1 + (groups - 1) + (owners - 1))
+
+    def remote(src, dst, s, r, to):
+        return pltpu.make_async_remote_copy(
+            src_ref=src, dst_ref=dst, send_sem=s, recv_sem=r, device_id=to, device_id_type=mesh_id
+        )
+
+    nears = []
+    for d in range(1, groups):
+        there = lax.rem(hi + d, groups)
+        for x, ref in enumerate((dkb_ref, dvb_ref)):
+            nears.append(
+                remote(
+                    ref.at[:, pl.ds(pl.multiple_of(there * bw, bw), bw)], near.at[d, x],
+                    near_s.at[d, x], near_r.at[d, x], {"tp": there * CORES + lo},
+                )
+            )
+    for cp in nears:
+        cp.start()
+
+    def back_copy(d, x):
+        ref = (dkp_ref, dvp_ref)[x]
+        return remote(
+            ref.at[pl.ds((d - 1) * rows, rows)], back.at[d, x], back_s.at[d, x], back_r.at[d, x],
+            {"tp": jnp.maximum(hi - d, 0) * CORES + lo},
+        )
+
+    for d in range(1, groups):
+
+        @pl.when(hi >= d)
+        def _(d=d):
+            for x in range(2):
+                back_copy(d, x).start()
+
+    def swap(x, src, dst, s, r, l):
+        width = src.shape[1] // groups
+        res = []
+        for j in range(groups):
+            cols = pl.ds(pl.multiple_of((CORES * j + lo) * width, width), width)
+            away = src.at[pl.ds(pl.multiple_of(other * tokens, tokens), tokens), pl.ds(j * width, width)]
+            here = src.at[pl.ds(pl.multiple_of(lo * tokens, tokens), tokens), pl.ds(j * width, width)]
+            res.append(
+                (
+                    remote(away, dst.at[:, cols], s.at[x, j], r.at[x, j], sibling),
+                    pltpu.make_async_copy(here, dst.at[:, cols], l.at[x, j]),
+                )
+            )
+        return res
+
+    swaps = swap(0, out_ref, tout_ref, tok_s, tok_r, tok_l) + swap(1, gq_ref, tgq_ref, tok_s, tok_r, tok_l)
+    for far, local in swaps:
+        far.start()
+        local.start()
+
+    for cp in nears:
+        cp.wait_recv()
+    mine = pl.ds(pl.multiple_of(hi * bw, bw), bw)
+    for x, ref in enumerate((dkb_ref, dvb_ref)):
+        acc = ref[:, mine].astype(F32)
+        for d in range(1, groups):
+            acc = acc + near[d, x].astype(F32)
+        part[x] = acc
+
+    def own_copy(d):
+        return remote(
+            send.at[d], got.at[d], own_s.at[d], own_r.at[d], {"ctx": jnp.maximum(me - d, 0)}
+        )
+
+    for d in range(owners - 1, 0, -1):
+
+        @pl.when(me >= d)
+        def _(d=d):
+            for x in range(2):
+                acc = jnp.zeros((block, bw), F32)
+                for j in range(slots):
+                    hit = jnp.logical_and(row_ref[0, j] == me - d, count_ref[0] > j)
+                    acc = acc + part[x, j * block : (j + 1) * block, :] * jnp.where(hit, 1.0, 0.0)
+                send[d, x] = acc.astype(BF)
+            own_copy(d).start()
+
+    summed[0] = dko_ref[...].astype(BF)
+    summed[1] = dvo_ref[...].astype(BF)
+    for d in range(1, groups):
+
+        @pl.when(hi + d < groups)
+        def _(d=d):
+            for x, ref in enumerate((dko_ref, dvo_ref)):
+                back_copy(d, x).wait_recv()
+                base = ref[...] if d == 1 else summed[x].astype(F32)
+                summed[x] = (base + back[d, x].astype(F32)).astype(BF)
+
+    kvs = swap(0, summed.at[0], tgk_ref, kv_s, kv_r, kv_l) + swap(1, summed.at[1], tgv_ref, kv_s, kv_r, kv_l)
+    for far, local in kvs:
+        far.start()
+        local.start()
+
+    part[:, :block, :] = jnp.zeros((2, block, bw), F32)
+    for d in range(1, owners):
+
+        @pl.when(me + d < owners)
+        def _(d=d):
+            own_copy(d).wait_recv()
+            part[:, :block, :] += got[d].astype(F32)
+
+    bk_ref[...] = part[0, :block, :].astype(BF)
+    bv_ref[...] = part[1, :block, :].astype(BF)
+    for far, local in swaps + kvs:
+        far.wait_recv()
+        far.wait_send()
+        local.wait()
+    for cp in nears:
+        cp.wait_send()
+    for d in range(1, groups):
+
+        @pl.when(hi >= d)
+        def _(d=d):
+            for x in range(2):
+                back_copy(d, x).wait_send()
+
+    for d in range(1, owners):
+
+        @pl.when(me >= d)
+        def _(d=d):
+            own_copy(d).wait_send()
+
+
+def deliver(row, count, out, gq, dko, dvo, dkp, dvp, dkb, dvb, groups, owners, tokens, bw):
+    slots = row.shape[1]
+    block = dkb.shape[0] // slots
+    rows, cols = dko.shape
+    vm = pl.BlockSpec(memory_space=pltpu.VMEM)
+    sm = pl.BlockSpec(memory_space=pltpu.SMEM)
+    hbm = pl.BlockSpec(memory_space=pl.ANY)
+    dma = pltpu.SemaphoreType.DMA
+    tok_q = jax.ShapeDtypeStruct((tokens, out.shape[1] * CORES), BF)
+    tok_k = jax.ShapeDtypeStruct((tokens, cols * CORES), BF)
+    bea = jax.ShapeDtypeStruct((block, bw), BF)
+    pair = dma((groups, 2))
+    two = dma((2, groups))
+    return pl.pallas_call(
+        functools.partial(deliver_kernel, groups, owners, slots),
+        out_shape=[tok_q, tok_q, tok_k, tok_k, bea, bea],
+        in_specs=[sm, sm, hbm, hbm] + [vm] * 6,
+        out_specs=[hbm, hbm, hbm, hbm, vm, vm],
+        scratch_shapes=[
+            pltpu.VMEM((groups, 2, slots * block, bw), BF),
+            pltpu.VMEM((groups, 2, rows, cols), BF),
+            pltpu.VMEM((2, rows, cols), BF),
+            pltpu.VMEM((2, slots * block, bw), F32),
+            pltpu.VMEM((owners, 2, block, bw), BF),
+            pltpu.VMEM((owners, 2, block, bw), BF),
+            pair, pair, pair, pair, two, two, two, two, two, two,
+            dma((owners,)), dma((owners,)),
+        ],
+        compiler_params=pltpu.CompilerParams(
+            collective_id=1, has_side_effects=True, vmem_limit_bytes=48 * 1024 * 1024
+        ),
+    )(row, count, out, gq, dko, dvo, dkp, dvp, dkb, dvb)
+
+
 def shards(
     queries, keys_in, values_in, grad_output, beacon_keys, beacon_values, read_blocks, read_counts
 ):
@@ -241,55 +428,11 @@
         count[None], hi[None].astype(jnp.int32), groups - 1, slots,
     )
 
-    def quarter(x, j):
-        return lax.dynamic_slice_in_dim(x, j * bw, bw, axis=1)
-
-    def both(j):
-        return jnp.concatenate([quarter(dkb, j), quarter(dvb, j)], axis=1)
-
-    beacon = both(hi).astype(F32)
-    for d in range(1, groups):
-        pairs = [(i, (i + CORES * d) % tp) for i in range(tp)]
-        beacon = beacon + lax.ppermute(both((hi + d) % groups), "tp", pairs).astype(F32)
-    beacon = beacon.reshape(slots, block_rows, 2 * bw)
-    used = jnp.arange(slots, dtype=jnp.int32) < count
-    ids = jnp.arange(owners, dtype=jnp.int32)
-    dense = jnp.zeros((owners, block_rows, 2 * bw), F32)
-    for j in range(slots):
-        hit = (ids == row[j]) & used[j]
-        dense = dense + jnp.where(hit[:, None, None], beacon[j][None], 0.0)
-    dense = dense.astype(BF).reshape(owners * block_rows, 2 * bw)
-    own_b = lax.psum_scatter(dense, "ctx", scatter_dimension=0, tiled=True)
-
-    rows_g = k.shape[0]
-    kvg = jnp.concatenate([dko, dvo], axis=1)
-    back = jnp.concatenate([dkp, dvp], axis=1)
-    for d in range(1, groups):
-        pairs = [(i + CORES * d, i) for i in range(tp - CORES * d)]
-        kvg = kvg + lax.ppermute(back[(d - 1) * rows_g : d * rows_g], "tp", pairs).astype(F32)
-    kvg = kvg.astype(BF)
-
-    def swap_out(*arrays):
-        send = jnp.concatenate(
-            [lax.dynamic_slice_in_dim(a, (1 - lo) * tokens, tokens, axis=0) for a in arrays], axis=1
-        )
-        got = lax.ppermute(send, "tp", sibling)
-        res, at = [], 0
-        for a in arrays:
-            n = a.shape[1]
-            keep = lax.dynamic_slice_in_dim(a, lo * tokens, tokens, axis=0)
-            new = got[:, at : at + n]
-            at += n
-            w = n // groups
-            cols = []
-            for j in range(groups):
-                cols.append(by_rank(keep[:, j * w : (j + 1) * w], new[:, j * w : (j + 1) * w], 1))
-            res.append(jnp.concatenate(cols, axis=1))
-        return res
-
-    tok_out, tok_gq = swap_out(out, gq)
-    tok_gk, tok_gv = swap_out(kvg[:, :half_cols], kvg[:, half_cols:])
-    return (tok_out, tok_gq, tok_gk, tok_gv, own_b[:, :bw], own_b[:, bw:])
+    return tuple(
+        deliver(
+            read_blocks, read_counts, out, gq, dko, dvo, dkp, dvp, dkb, dvb, groups, owners, tokens, bw
+        )
+    )
 
 
 def solution(mesh):

time: 243 us -> 222 us (0.914)
  waiting for transfers between devices: 110 us -> 37.3 us
  Pallas kernels: 63.8 us -> 131 us
  other arithmetic: 32.3 us -> 12.3 us
  local copies, waits for them, and re-layouts: 11.8 us -> 18.9 us
  starting transfers between devices: 5.24 us -> 2.44 us
    pallas_call x0 -> x1, Pallas kernels: none -> 67 us  [deliver(): pl.pallas_call(functools.partial(deliver_kernel, groups, owners, slots),...]
    reduce_scatter x1 -> x0, waiting for transfers between devices: 56.5 us -> none  [shards(): own_b = lax.psum_scatter(dense, 'ctx', scatter_dimension=0, tiled=True)]
    ppermute x4 -> x0, waiting for transfers between devices: 28.7 us -> none  [the longest x1 21.7 us: shards(): lax.ppermute(back[(d - 1) * rows_g:d * rows_g], 'tp', pairs).astype(F32)]
    unnamed x20 -> x26, local copies, waits for them, and re-layouts: 0.04 us -> 9.92 us
    all_gather x1, waiting for transfers between devices: 0.01 us -> 8.69 us  [shards(): lax.all_gather(jnp.concatenate([beacon_keys, beacon_values], axis=1), 'ct...]
    concatenate x8 -> x0, other arithmetic: 7.26 us -> none  [the longest x4 4.7 us: swap_out(): res.append(jnp.concatenate(cols, axis=1))]
    and x4 -> x0, other arithmetic: 4.92 us -> none  [shards(): hit = (ids == row[j]) & used[j]]
    select_n x4 -> x2, other arithmetic: 8.18 us -> 3.85 us  [by_rank(): first = jnp.where(lo == 0, mine, theirs)]
  transfers between devices with their start and end apart: 10 -> 5, of which waited for: 5 -> 3; matrix products, arithmetic and copies ran while one was open for 16% -> 8% of each run, Pallas kernels for 0% -> 0%
where the time goes in v3:
time: 222 us; the launch traced here: 219 us
  Pallas kernels  131 us (59%)
  waiting for transfers between devices  37.3 us (17%)
  local copies, waits for them, and re-layouts  18.9 us (9%)
  between operations  17.4 us (8%)
  other arithmetic  12.3 us (6%)
  starting transfers between devices  2.44 us (1%)
    pallas_call x1, Pallas kernels, deliver(): pl.pallas_call(functools.partial(deliver_kernel, groups, owners, slots),...  67 us
    pallas_call x1, Pallas kernels, attention(): pl.pallas_call(functools.partial(attention_kernel, group, prev_groups, sl...  63.7 us
    ppermute x1, waiting for transfers between devices, shards(): prevs.append(lax.ppermute(kv, 'tp', pairs))  22 us
    unnamed x26, local copies, waits for them, and re-layouts  9.92 us
    all_gather x1, waiting for transfers between devices, shards(): lax.all_gather(jnp.concatenate([beacon_keys, beacon_values], axis=1), 'ct...  8.69 us
    ppermute x1, waiting for transfers between devices, shards(): quarters.append(lax.ppermute(mine, 'tp', pairs))  6.65 us
    dynamic_slice x2, local copies, waits for them, and re-layouts, column_half(): lax.dynamic_slice_in_dim(x, (CORES * j + which) * w, w, axis=1)  5.1 us
  transfers between devices with their start and end apart: 5, of which 3 were waited for; matrix products, arithmetic and copies ran while one was open for 8% of the time, Pallas kernels for 0%

profile of v3, /device:TPU:12, one launch (start us, length us, event | category | flops | bytes accessed | tf_op | source)
XLA Modules:
  0.0 219.2 jit_solution(18371906614143851251)
XLA Ops:
  7.2 0.0 copy-start.3
  7.2 0.0 all-gather.2.cloned.1.call-start
  7.2 2.2 constant_dynamic-slice_fusion.5
  9.4 0.9 pad_maximum_fusion.5
  10.3 0.0 collective-permute-start.1
  10.3 0.0 copy-done.3
  10.3 2.9 %constant_dynamic-slice_fusion.13 = (bf16[256,1024]{1,0:T(8,128)(2,1)S(1)}, bf16[256,1024]{1,0:T(8,128)(2,1)S(1)}, bf16[256,1024]{1,0:T(8,128)(2,1)S(1)}, bf16[2...) fusion(bf16[256,4096]{1,0:T(8,128)(2,1)S(1)} %copy-done.3, ...), kind=kLoop, calls=%fused_computation.40 | loop fusion | bytes 8388624 | tf_op jit(solution)/shard_map/dynamic_slice | solution.py:373
  13.2 1.5 pad_maximum_fusion
  14.7 0.5 collective-permute-start
  15.2 0.0 copy-done.8
  15.2 0.0 copy-done.9
  15.2 0.7 pad_maximum_fusion.13
  15.9 0.0 all-gather.2.cloned.1.call-update
  15.9 0.0 collective-permute-done.1
  15.9 0.0 copy-done.7
  15.9 0.0 copy-start.2
  16.0 1.2 broadcast_select_fusion.9
  17.2 1.1 maximum_maximum_fusion
  18.3 1.3 collective-permute-start.2
  19.6 0.0 copy-done.2
  19.6 0.7 fusion.1
  23.6 0.0 copy-start.4
  23.6 22.0 %collective-permute-done.2 = bf16[512,1024]{1,0:T(8,128)(2,1)} collective-permute-done((bf16[512,1024]{1,0:T(8,128)(2,1)}, bf16[512,1024]{1,0:T(8,128)(2,1)}, u32[]{:S(2)}, u32[]{:S(2)}) %collective-permute-start.2) | collective-permute-done | bytes 1048608 | tf_op jit(solution)/shard_map/ppermute | solution.py:402
  45.6 2.1 fusion
  47.6 8.7 %all-gather.2.cloned.1.call-done = bf16[1024,512]{1,0:T(8,128)(2,1)} async-done(((bf16[128,512]{1,0:T(8,128)(2,1)}), bf16[1024,512]{1,0:T(8,128)(2,1)}) %all-gather.2.cloned.1.call-update) | async-done | bytes 1048592 | tf_op jit(solution)/shard_map/all_gather | solution.py:394
  56.3 1.2 constant_dynamic-slice_fusion.3
  57.6 0.6 collective-permute-start.3
  58.2 0.0 collective-permute-done
  58.2 0.0 copy-done.4
  58.2 0.0 copy-done.5
  58.2 2.6 %broadcast_select_fusion.1 = (bf16[256,2048]{1,0:T(8,128)(2,1)S(1)}, bf16[256,2048]{1,0:T(8,128)(2,1)S(1)}, bf16[256,2048]{1,0:T(8,128)(2,1)S(1)}, bf16[256,2048]{1,0:T(8,128)(2,1)S(1)}) fusion(pred[]{:T(512)S(6)} %eq.12, bf16[256,4096]{1,0:T(8,128)(2,1)} %collective-permute-done, bf16[256,1024]{1,0:T(8,128)(2,1)S(1)} %get-tuple-element.31, ...), kind=kLoop, calls=%fused_computation.7 | loop fusion | flops 6291456 | bytes 8388609 | tf_op jit(solution)/shard_map/jit(_where)/select_n | solution.py:380
  60.8 1.6 pad_maximum_fusion.2.g_ref
  62.4 1.6 pad_maximum_fusion.1.q_ref
  64.0 6.7 %collective-permute-done.3 = bf16[512,512]{1,0:T(8,128)(2,1)S(1)} collective-permute-done((bf16[512,512]{1,0:T(8,128)(2,1)S(1)}, bf16[512,512]{1,0:T(8,128)(2,1)S(1)}, u32[]{:S(2)}, u32[]{:S(2)}) %collective-permute-start.3) | collective-permute-done | bytes 524320 | tf_op jit(solution)/shard_map/ppermute | solution.py:414
  70.6 0.1 broadcast_select_fusion.6
  70.7 1.0 pad_maximum_fusion.9
  71.7 63.7 %shard_map.127 = (bf16[512,2048]{1,0:T(8,128)(2,1)}, bf16[512,2048]{1,0:T(8,128)(2,1)}, f32[512,512]{1,0:T(8,128)}, f32[512,512]{1,0:T(8,128)}, bf16[512,512]{1,...) custom-call(s32[1]{0:T(128)S(6)} %copy.20.count_ref, ...), custom_call_target="tpu_custom_call" | custom-call | flops 19327352832 | bytes 8388608 | tf_op jit(solution)/shard_map/pallas_call | solution.py:144
  135.5 1.2 copy-done
  136.7 1.2 copy-done.1
  137.9 67.0 %shard_map.128 = (bf16[256,4096]{1,0:T(8,128)(2,1)}, bf16[256,4096]{1,0:T(8,128)(2,1)}, bf16[256,1024]{1,0:T(8,128)(2,1)S(1)}, bf16[256,1024]{1,0:T(8,128)(2,1)S...) custom-call(s32[1,4]{1,0:T(1,128)S(1)} %copy-done.2, s32[1]{0:T(128)S(6)} %copy.20.count_ref, ...), custom_call_target="tpu_custom_call" | custom-call | tf_op jit(solution)/shard_map/pallas_call | solution.py:336
  204.9 0.0 copy-start.6
  204.9 3.3 %copy.21 = bf16[256,4096]{1,0:T(8,128)(2,1)} copy(bf16[256,4096]{1,0:T(8,128)(2,1)} %get-tuple-element.80) | data formatting | bytes 4194304
  208.2 0.0 copy-done.6
  208.2 1.3 copy.22
  209.5 0.8 copy.23
  210.3 0.8 copy.24
  211.1 0.6 copy.25
  211.7 0.6 copy.26
  (9 shorter events, 0.1 us)
Async XLA Ops:
  7.2 3.1 %copy-start.3 = (bf16[256,4096]{1,0:T(8,128)(2,1)S(1)}, bf16[256,4096]{1,0:T(8,128)(2,1)}, u32[]{:S(2)}) copy-start(bf16[256,4096]{1,0:T(8,128)(2,1)} %param.11) | copy-start | bytes 6291460
  7.2 49.2 %all-gather.2.cloned.1.call-start = ((), (), s32[]{:S(2)}) async-start(), calls=%async_computation | async-start | bytes 1179648 | tf_op jit(solution)/shard_map/all_gather | solution.py:394
  10.3 5.7 %collective-permute-start.1 = (bf16[256,1024]{1,0:T(8,128)(2,1)}, bf16[256,1024]{1,0:T(8,128)(2,1)}, u32[]{:S(2)}, u32[]{:S(2)}) collective-permute-start(bf16[256,1024]{1,0:T(8,128)(2,1)} %pad_maximum_fusion.5), channel_id=1, source_target_pairs={{0,1},{1,0},{2,3},{3,2},{4,5},{5,4},{6,7},{7,6},{8,9},{9,8},{10,11... | collective-permute-start | bytes 1572872 | tf_op jit(solution)/shard_map/ppermute | solution.py:387
  13.2 2.0 copy-start.8
  13.2 2.0 copy-start.9
  13.2 2.7 %copy-start.7 = (bf16[256,256]{1,0:T(8,128)(2,1)S(1)}, bf16[256,256]{1,0:T(8,128)(2,1)}, u32[]{:S(2)}) copy-start(bf16[256,256]{1,0:T(8,128)(2,1)} %get-tuple-element.71) | copy-start | bytes 393220
  14.7 43.5 %collective-permute-start = (bf16[256,4096]{1,0:T(8,128)(2,1)}, bf16[256,4096]{1,0:T(8,128)(2,1)}, u32[]{:S(2)}, u32[]{:S(2)}) collective-permute-start(bf16[256,4096]{1,0:T(8,128)(2,1)} %pad_maximum_fusion), channel_id=1, source_target_pairs={{0,1},{1,0},{2,3},{3,2},{4,5},{5,4},{6,7},{7,6},{8,9},{9,8},{10,11... | collective-permute-start | bytes 6291464 | tf_op jit(solution)/shard_map/ppermute | solution.py:387
  15.9 3.7 %copy-start.2 = (s32[1,4]{1,0:T(1,128)S(1)}, s32[1,4]{1,0:T(1,128)}, u32[]{:S(2)}) copy-start(s32[1,4]{1,0:T(1,128)} %row_ref.1) | copy-start | bytes 52
  18.3 27.3 %collective-permute-start.2 = (bf16[512,1024]{1,0:T(8,128)(2,1)}, bf16[512,1024]{1,0:T(8,128)(2,1)}, u32[]{:S(2)}, u32[]{:S(2)}) collective-permute-start(bf16[512,1024]{1,0:T(8,128)(2,1)} %maximum_maximum_fusion), channel_id=1, source_target_pairs={{0,2},{1,3},{4,6},{5,7},{8,10},{9,11},{12,14},{13,15},{16,18},{17,... | collective-permute-start | bytes 3145736 | tf_op jit(solution)/shard_map/ppermute | solution.py:402
  23.6 34.6 %copy-start.4 = (bf16[256,1024]{1,0:T(8,128)(2,1)S(1)}, bf16[256,1024]{1,0:T(8,128)(2,1)}, u32[]{:S(2)}) copy-start(bf16[256,1024]{1,0:T(8,128)(2,1)} %get-tuple-element.66) | copy-start | bytes 1572868
  56.3 1.9 copy-start.5
  57.6 13.1 %collective-permute-start.3 = (bf16[512,512]{1,0:T(8,128)(2,1)S(1)}, bf16[512,512]{1,0:T(8,128)(2,1)S(1)}, u32[]{:S(2)}, u32[]{:S(2)}) collective-permute-start(bf16[512,512]{1,0:T(8,128)(2,1)S(1)} %pad_maximum_fusion.8), channel_id=1, source_target_pairs={{0,2},{1,3},{2,0},{3,1},{4,6},{5,7},{6,4},{7,5},{8,10},{9,11},{10,... | collective-permute-start | bytes 1572872 | tf_op jit(solution)/shard_map/ppermute | solution.py:414
  135.5 1.2 copy-start
  136.7 1.2 copy-start.1
  204.9 3.3 %copy-start.6 = (bf16[256,4096]{1,0:T(8,128)(2,1)S(1)}, bf16[256,4096]{1,0:T(8,128)(2,1)}, u32[]{:S(2)}) copy-start(bf16[256,4096]{1,0:T(8,128)(2,1)} %get-tuple-element.81) | copy-start | bytes 6291460
Sparse Core Ops, SparseCore 0:
  16.0 40.2 all-gather.1

commit v4 on v2

--- a/solution.py
+++ b/solution.py
@@ -227,6 +227,9 @@
         compiler_params=pltpu.CompilerParams(
             collective_id=1, has_side_effects=True, vmem_limit_bytes=32 * 1024 * 1024
         ),
+        cost_estimate=pl.CostEstimate(
+            flops=dense.size, bytes_accessed=2 * owners * dense.size * 2, transcendentals=0
+        ),
     )(dense)
 
 
@@ -311,9 +314,12 @@
         return jnp.concatenate([quarter(dkb, j), quarter(dvb, j)], axis=1)
 
     beacon = both(hi).astype(F32)
+    back = jnp.concatenate([dkp, dvp], axis=1)
     for d in range(1, groups):
         pairs = [(i, (i + CORES * d) % tp) for i in range(tp)]
-        beacon = beacon + lax.ppermute(both((hi + d) % groups), "tp", pairs).astype(F32)
+        there = lax.ppermute(both((hi + d) % groups), "tp", pairs)
+        back, there = lax.optimization_barrier((back, there))
+        beacon = beacon + there.astype(F32)
     beacon = beacon.reshape(slots, block_rows, 2 * bw)
     used = jnp.arange(slots, dtype=jnp.int32) < count
     ids = jnp.arange(owners, dtype=jnp.int32)
@@ -326,10 +332,11 @@
 
     rows_g = k.shape[0]
     kvg = jnp.concatenate([dko, dvo], axis=1)
-    back = jnp.concatenate([dkp, dvp], axis=1)
     for d in range(1, groups):
         pairs = [(i + CORES * d, i) for i in range(tp - CORES * d)]
-        kvg = kvg + lax.ppermute(back[(d - 1) * rows_g : d * rows_g], "tp", pairs).astype(F32)
+        term = lax.ppermute(back[(d - 1) * rows_g : d * rows_g], "tp", pairs)
+        term, own_b = lax.optimization_barrier((term, own_b))
+        kvg = kvg + term.astype(F32)
     kvg = kvg.astype(BF)
 
     def swap_out(*arrays):

time: 208 us -> 195 us (0.938)
  the two profiles are of different devices: /device:TPU:11 before, /device:TPU:12 now
where the time goes in v4:
time: 195 us; the launch traced here: 192 us
  Pallas kernels  88.9 us (46%)
  waiting for transfers between devices  37.1 us (19%)
  other arithmetic  31.3 us (16%)
  between operations  17.6 us (9%)
  local copies, waits for them, and re-layouts  11.6 us (6%)
  starting transfers between devices  5.59 us (3%)
    pallas_call x1, Pallas kernels, attention(): pl.pallas_call(functools.partial(attention_kernel, group, prev_groups, sl...  63.7 us
    pallas_call x1, Pallas kernels, to_owners(): pl.pallas_call(owners_kernel, out_shape=jax.ShapeDtypeStruct((block, widt...  25.1 us
    ppermute x1, waiting for transfers between devices, shards(): prevs.append(lax.ppermute(kv, 'tp', pairs))  17.7 us
    ppermute x1, waiting for transfers between devices, shards(): there = lax.ppermute(both((hi + d) % groups), 'tp', pairs)  10.6 us
    select_n x4, other arithmetic, by_rank(): first = jnp.where(lo == 0, mine, theirs)  8.02 us
    ppermute x1, waiting for transfers between devices, shards(): quarters.append(lax.ppermute(mine, 'tp', pairs))  6.66 us
    dynamic_slice x2, local copies, waits for them, and re-layouts, column_half(): lax.dynamic_slice_in_dim(x, (CORES * j + which) * w, w, axis=1)  5.11 us
    and x4, other arithmetic, shards(): hit = (ids == row[j]) & used[j]  4.89 us
  transfers between devices with their start and end apart: 9, of which 5 were waited for; matrix products, arithmetic and copies ran while one was open for 17% of the time, Pallas kernels for 13%

profile of v4, /device:TPU:12, one launch (start us, length us, event | category | flops | bytes accessed | tf_op | source)
XLA Modules:
  0.0 192.0 jit_solution(16015450783230252846)
XLA Ops:
  7.2 1.7 pad_maximum_fusion.21
  9.0 2.0 %constant_dynamic-slice_fusion.13 = (bf16[256,256]{1,0:T(8,128)(2,1)S(1)}, bf16[256,256]{1,0:T(8,128)(2,1)S(1)}, bf16[256,256]{1,0:T(8,128)(2,1)S(1)}, bf16[256,...) fusion(bf16[256,1024]{1,0:T(8,128)(2,1)} %param.10, ...), kind=kLoop, calls=%fused_computation.75 | loop fusion | bytes 2097168 | tf_op jit(solution)/shard_map/dynamic_slice | solution.py:252
  11.0 0.9 pad_maximum_fusion.9
  11.8 3.1 %constant_dynamic-slice_fusion.21 = (bf16[256,1024]{1,0:T(8,128)(2,1)S(1)}, bf16[256,1024]{1,0:T(8,128)(2,1)S(1)}, bf16[256,1024]{1,0:T(8,128)(2,1)S(1)}, bf16[2...) fusion(bf16[256,4096]{1,0:T(8,128)(2,1)S(1)} %copy-done, ...), kind=kLoop, calls=%fused_computation.83 | loop fusion | bytes 8388624 | tf_op jit(solution)/shard_map/dynamic_slice | solution.py:252
  14.9 1.5 pad_maximum_fusion
  16.4 0.5 collective-permute-start
  16.9 0.7 fusion.10
  18.3 1.2 broadcast_select_fusion.17
  19.5 1.1 maximum_maximum_fusion
  20.6 1.3 collective-permute-start.2
  24.5 0.6 fusion.9
  25.1 1.3 compare_and_fusion
  26.4 1.2 compare_and_fusion.1
  27.7 1.2 compare_and_fusion.2
  28.8 1.2 compare_and_fusion.3
  30.0 0.1 broadcast_bitcast_fusion
  30.2 17.7 %collective-permute-done.2 = bf16[512,1024]{1,0:T(8,128)(2,1)} collective-permute-done((bf16[512,1024]{1,0:T(8,128)(2,1)}, bf16[512,1024]{1,0:T(8,128)(2,1)}, u32[]{:S(2)}, u32[]{:S(2)}) %collective-permute-start.2) | collective-permute-done | bytes 1048608 | tf_op jit(solution)/shard_map/ppermute | solution.py:281
  47.9 2.1 %fusion.7 = (bf16[512,512]{1,0:T(8,128)(2,1)}, bf16[512,512]{1,0:T(8,128)(2,1)S(1)}) fusion(bf16[512,1024]{1,0:T(8,128)(2,1)} %collective-permute-done.2), kind=kLoop, calls=%fused_computation.101 | loop fusion | bytes 2097152 | tf_op jit(solution)/shard_map/slice | solution.py:306
  50.0 0.5 all-gather.2.cloned.1.call-done
  50.5 1.2 constant_dynamic-slice_fusion.11
  51.7 0.6 collective-permute-start.3
  52.4 2.6 %broadcast_select_fusion.1 = (bf16[256,2048]{1,0:T(8,128)(2,1)S(1)}, bf16[256,2048]{1,0:T(8,128)(2,1)S(1)}, bf16[256,2048]{1,0:T(8,128)(2,1)S(1)}, bf16[256,2048]{1,0:T(8,128)(2,1)S(1)}) fusion(pred[]{:T(512)S(6)} %eq.81, bf16[256,4096]{1,0:T(8,128)(2,1)} %collective-permute-done, bf16[256,1024]{1,0:T(8,128)(2,1)S(1)} %get-tuple-element.51, ...), kind=kLoop, calls=%fused_computation.22 | loop fusion | flops 6291456 | bytes 8388609 | tf_op jit(solution)/shard_map/jit(_where)/select_n | solution.py:259
  55.0 1.6 pad_maximum_fusion.2.g_ref
  56.5 1.6 pad_maximum_fusion.1.q_ref
  58.1 6.7 %collective-permute-done.3 = bf16[512,512]{1,0:T(8,128)(2,1)S(1)} collective-permute-done((bf16[512,512]{1,0:T(8,128)(2,1)S(1)}, bf16[512,512]{1,0:T(8,128)(2,1)S(1)}, u32[]{:S(2)}, u32[]{:S(2)}) %collective-permute-start.3) | collective-permute-done | bytes 524320 | tf_op jit(solution)/shard_map/ppermute | solution.py:293
  64.9 1.0 pad_maximum_fusion.13
  65.9 63.7 %shard_map.127 = (bf16[512,2048]{1,0:T(8,128)(2,1)}, bf16[512,2048]{1,0:T(8,128)(2,1)}, f32[512,512]{1,0:T(8,128)}, f32[512,512]{1,0:T(8,128)}, bf16[512,512]{1,...) custom-call(s32[1]{0:T(128)} %copy.14.count_ref, ...), custom_call_target="tpu_custom_call" | custom-call | flops 19327352832 | bytes 8388608 | tf_op jit(solution)/shard_map/pallas_call | solution.py:144
  129.8 0.6 collective-permute-start.5
  130.5 0.1 pad_maximum_fusion.8
  130.6 0.6 copy-done.1
  131.3 10.6 %collective-permute-done.5 = bf16[512,512]{1,0:T(8,128)(2,1)S(1)} collective-permute-done((bf16[512,512]{1,0:T(8,128)(2,1)S(1)}, bf16[512,512]{1,0:T(8,128)(2,1)S(1)}, u32[]{:S(2)}, u32[]{:S(2)}) %collective-permute-start.5) | collective-permute-done | bytes 524320 | tf_op jit(solution)/shard_map/ppermute | solution.py:320
  141.9 2.5 %collective-permute-start.6 = (bf16[512,1024]{1,0:T(8,128)(2,1)S(1)}, bf16[512,1024]{1,0:T(8,128)(2,1)S(1)}, u32[]{:S(2)}, u32[]{:S(2)}) collective-permute-start(bf16[512,1024]{1,0:T(8,128)(2,1)S(1)} %pad_maximum_fusion.8), channel_id=1, source_target_pairs={{2,0},{3,1},{6,4},{7,5},{10,8},{11,9},{14,12},{15,13},{18,16},{19,... | collective-permute-start | bytes 3145736 | tf_op jit(solution)/shard_map/ppermute | solution.py:337
  144.4 0.1 constant_dynamic-slice_fusion.6
  144.6 1.5 pad_maximum_fusion.3
  146.1 0.2 convert_add_fusion
  146.4 1.1 fusion.2.dense_ref
  147.5 25.1 %shard_map.128 = bf16[128,512]{1,0:T(8,128)(2,1)S(1)} custom-call(bf16[1024,512]{1,0:T(8,128)(2,1)S(1)} %fusion.2.dense_ref), custom_call_target="tpu_custom_call" | custom-call | flops 524288 | bytes 16777216 | tf_op jit(solution)/shard_map/pallas_call | solution.py:216
  172.6 0.3 fusion
  173.0 0.1 fusion.5
  173.1 0.9 pad_maximum_fusion.16
  174.0 0.7 fusion.8
  174.7 1.6 collective-permute-done.7
  176.2 1.3 broadcast_select_fusion.23
  177.6 0.9 pad_maximum_fusion.18
  178.4 0.9 pad_maximum_fusion.17
  179.3 2.9 %broadcast_select_fusion.7 = (bf16[256,1024]{1,0:T(8,128)(2,1)S(1)}, bf16[256,1024]{1,0:T(8,128)(2,1)S(1)}, bf16[256,1024]{1,0:T(8,128)(2,1)S(1)}, bf16[256,1024...) fusion(pred[]{:T(512)S(6)} %eq.81, ...), kind=kLoop, calls=%fused_computation.38 | loop fusion | flops 2097152 | bytes 8388617 | tf_op jit(solution)/shard_map/jit(_where)/select_n | solution.py:259
  182.2 1.5 pad_maximum_fusion.5
  183.7 1.5 pad_maximum_fusion.4
  (41 shorter events, 0.7 us)
Async XLA Ops:
  7.2 4.7 %copy-start = (bf16[256,4096]{1,0:T(8,128)(2,1)S(1)}, bf16[256,4096]{1,0:T(8,128)(2,1)}, u32[]{:S(2)}) copy-start(bf16[256,4096]{1,0:T(8,128)(2,1)} %param.11) | copy-start | bytes 6291460
  7.2 43.3 %all-gather.2.cloned.1.call-start = ((), (), s32[]{:S(2)}) async-start(), calls=%async_computation | async-start | bytes 1179648 | tf_op jit(solution)/shard_map/all_gather | solution.py:273
  11.8 6.4 %collective-permute-start.1 = (bf16[256,1024]{1,0:T(8,128)(2,1)}, bf16[256,1024]{1,0:T(8,128)(2,1)}, u32[]{:S(2)}, u32[]{:S(2)}) collective-permute-start(bf16[256,1024]{1,0:T(8,128)(2,1)} %pad_maximum_fusion.9), channel_id=1, source_target_pairs={{0,1},{1,0},{2,3},{3,2},{4,5},{5,4},{6,7},{7,6},{8,9},{9,8},{10,11... | collective-permute-start | bytes 1572872 | tf_op jit(solution)/shard_map/ppermute | solution.py:266
  14.9 2.0 %copy-start.9 = (s32[1,4]{1,0:T(1,128)S(1)}, s32[1,4]{1,0:T(1,128)}, u32[]{:S(2)}) copy-start(s32[1,4]{1,0:T(1,128)} %param.14) | copy-start | bytes 52
  14.9 3.3 %copy-start.8 = (bf16[256,256]{1,0:T(8,128)(2,1)S(1)}, bf16[256,256]{1,0:T(8,128)(2,1)}, u32[]{:S(2)}) copy-start(bf16[256,256]{1,0:T(8,128)(2,1)} %get-tuple-element.119) | copy-start | bytes 393220
  16.4 35.9 %collective-permute-start = (bf16[256,4096]{1,0:T(8,128)(2,1)}, bf16[256,4096]{1,0:T(8,128)(2,1)}, u32[]{:S(2)}, u32[]{:S(2)}) collective-permute-start(bf16[256,4096]{1,0:T(8,128)(2,1)} %pad_maximum_fusion), channel_id=1, source_target_pairs={{0,1},{1,0},{2,3},{3,2},{4,5},{5,4},{6,7},{7,6},{8,9},{9,8},{10,11... | collective-permute-start | bytes 6291464 | tf_op jit(solution)/shard_map/ppermute | solution.py:266
  20.6 27.3 %collective-permute-start.2 = (bf16[512,1024]{1,0:T(8,128)(2,1)}, bf16[512,1024]{1,0:T(8,128)(2,1)}, u32[]{:S(2)}, u32[]{:S(2)}) collective-permute-start(bf16[512,1024]{1,0:T(8,128)(2,1)} %maximum_maximum_fusion), channel_id=1, source_target_pairs={{0,2},{1,3},{4,6},{5,7},{8,10},{9,11},{12,14},{13,15},{16,18},{17,... | collective-permute-start | bytes 3145736 | tf_op jit(solution)/shard_map/ppermute | solution.py:281
  30.2 22.2 %copy-start.4 = (bf16[256,1024]{1,0:T(8,128)(2,1)S(1)}, bf16[256,1024]{1,0:T(8,128)(2,1)}, u32[]{:S(2)}) copy-start(bf16[256,1024]{1,0:T(8,128)(2,1)} %get-tuple-element.114) | copy-start | bytes 1572868
  50.5 1.9 copy-start.5
  51.7 13.1 %collective-permute-start.3 = (bf16[512,512]{1,0:T(8,128)(2,1)S(1)}, bf16[512,512]{1,0:T(8,128)(2,1)S(1)}, u32[]{:S(2)}, u32[]{:S(2)}) collective-permute-start(bf16[512,512]{1,0:T(8,128)(2,1)S(1)} %pad_maximum_fusion.12), channel_id=1, source_target_pairs={{0,2},{1,3},{2,0},{3,1},{4,6},{5,7},{6,4},{7,5},{8,10},{9,11},{10,... | collective-permute-start | bytes 1572872 | tf_op jit(solution)/shard_map/ppermute | solution.py:293
  129.7 1.6 copy-start.1
  129.8 12.1 %collective-permute-start.5 = (bf16[512,512]{1,0:T(8,128)(2,1)S(1)}, bf16[512,512]{1,0:T(8,128)(2,1)S(1)}, u32[]{:S(2)}, u32[]{:S(2)}) collective-permute-start(bf16[512,512]{1,0:T(8,128)(2,1)S(1)} %pad_maximum_fusion.15), channel_id=1, source_target_pairs={{0,2},{1,3},{2,0},{3,1},{4,6},{5,7},{6,4},{7,5},{8,10},{9,11},{10,... | collective-permute-start | bytes 1572872 | tf_op jit(solution)/shard_map/ppermute | solution.py:320
  130.5 14.0 %copy-start.2 = (bf16[512,2048]{1,0:T(8,128)(2,1)S(1)}, bf16[512,2048]{1,0:T(8,128)(2,1)}, u32[]{:S(2)}) copy-start(bf16[512,2048]{1,0:T(8,128)(2,1)} %get-tuple-element.19) | copy-start | bytes 6291460
  141.9 30.7 %collective-permute-start.6 = (bf16[512,1024]{1,0:T(8,128)(2,1)S(1)}, bf16[512,1024]{1,0:T(8,128)(2,1)S(1)}, u32[]{:S(2)}, u32[]{:S(2)}) collective-permute-start(bf16[512,1024]{1,0:T(8,128)(2,1)S(1)} %pad_maximum_fusion.8), channel_id=1, source_target_pairs={{2,0},{3,1},{6,4},{7,5},{10,8},{11,9},{14,12},{15,13},{18,16},{19,... | collective-permute-start | bytes 3145736 | tf_op jit(solution)/shard_map/ppermute | solution.py:337
  146.1 33.2 %collective-permute-start.4 = (bf16[256,4096]{1,0:T(8,128)(2,1)}, bf16[256,4096]{1,0:T(8,128)(2,1)}, u32[]{:S(2)}, u32[]{:S(2)}) collective-permute-start(bf16[256,4096]{1,0:T(8,128)(2,1)} %pad_maximum_fusion.3), channel_id=1, source_target_pairs={{0,1},{1,0},{2,3},{3,2},{4,5},{5,4},{6,7},{7,6},{8,9},{9,8},{10,11... | collective-permute-start | bytes 6291464 | tf_op jit(solution)/shard_map/ppermute | solution.py:346
  146.3 26.3 %copy-start.6 = (f32[512,512]{1,0:T(8,128)S(1)}, f32[512,512]{1,0:T(8,128)}, u32[]{:S(2)}) copy-start(f32[512,512]{1,0:T(8,128)} %get-tuple-element.20) | copy-start | bytes 3145732
  146.3 26.3 %copy-start.7 = (f32[512,512]{1,0:T(8,128)S(1)}, f32[512,512]{1,0:T(8,128)}, u32[]{:S(2)}) copy-start(f32[512,512]{1,0:T(8,128)} %get-tuple-element.21) | copy-start | bytes 3145732
  174.0 2.3 %collective-permute-start.7 = (bf16[256,1024]{1,0:T(8,128)(2,1)}, bf16[256,1024]{1,0:T(8,128)(2,1)}, u32[]{:S(2)}, u32[]{:S(2)}) collective-permute-start(bf16[256,1024]{1,0:T(8,128)(2,1)} %pad_maximum_fusion.16), channel_id=1, source_target_pairs={{0,1},{1,0},{2,3},{3,2},{4,5},{5,4},{6,7},{7,6},{8,9},{9,8},{10,11... | collective-permute-start | bytes 1572872 | tf_op jit(solution)/shard_map/ppermute | solution.py:346
  174.7 4.6 %copy-start.3 = (bf16[512,2048]{1,0:T(8,128)(2,1)S(1)}, bf16[512,2048]{1,0:T(8,128)(2,1)}, u32[]{:S(2)}) copy-start(bf16[512,2048]{1,0:T(8,128)(2,1)} %get-tuple-element.19) | copy-start | bytes 6291460
Sparse Core Ops, SparseCore 0:
  10.1 40.3 all-gather.1
